TPU v7x, 768 devices: a whole 4x8x12 slice. The times are simulated.
768 devices in a mesh: dom: 96 (over z, x, core), grp: 8 (over y).
Axes of the slice: x: 4, y: 8, z: 12, core: 2. Of those that a mesh axis runs over, the one named last changes fastest.
Arguments:
- fields: float32 [6, 20, 393216], P(None, None, ('dom', 'grp')), may hold values from -6 to 6
- section_res: float32 [6, 20, 393216], P(None, None, ('dom', 'grp')), may hold values from -6 to 6
- derivative: float32 [3, 20, 20], replicated, may hold values from -1.25 to 1.25
- geometry: float32 [9, 393216], P(None, ('dom', 'grp')), may hold values from -6 to 6
- normals: float32 [3, 4, 393216], P(None, None, ('dom', 'grp')), may hold values from -6 to 6
- face_scale: float32 [4, 393216], P(None, ('dom', 'grp')), may hold values from 0.5 to 2
- lift_matrix: float32 [20, 40], replicated, may hold values from -1 to 1
- interp_q: float32 [23, 20], replicated, may hold values from -1.25 to 1.25
- project_q: float32 [20, 23], replicated, may hold values from -1.25 to 1.25
- mat_table: float32 [2, 6], replicated, may hold values from 0.2 to 1
- materials: int32 [393216], P(('dom', 'grp')), may hold values from 0 to 5
- profile: float32 [2, 23, 393216], P(None, None, ('dom', 'grp')), may hold values from 0.5 to 2
- face_partner: int32 [4, 393216], P(None, ('dom', 'grp')), may hold values from 0 to 2303, as said below
- send_faces: int32 [2, 98304], P(None, ('dom', 'grp')), may hold values from -1 to 2047, as said below
- spectra: float32 [32, 12, 24576], P(None, None, ('dom', 'grp')), may hold values from -6 to 6
- huy_slots: int32 [24576], P(('dom', 'grp')), may hold values from 0 to 2047, as said below
- huy_worker: int32 [24576, 1], P(('dom', 'grp')), may hold values from 0 to 7; in each aligned block of 32 rows (0 to 31, 32 to 63, ...) at most 8 rows name the same one
- huy_pos: float32 [3, 24576], P(None, ('dom', 'grp')), may hold values from -4 to 4
- wavenumber: float32 [32], replicated, may hold values from 1 to 6
- time_phase: float32 [32], replicated, may hold values from -3.140625 to 3.140625
Outputs:
- new_fields: float32 [6, 20, 393216], P(None, None, ('dom', 'grp'))
- new_res: float32 [6, 20, 393216], P(None, None, ('dom', 'grp'))
- new_spectra: float32 [32, 12, 24576], P(None, None, ('dom', 'grp'))
- worker_spectra: float32 [32, 12, 49152], P(None, None, ('dom', 'grp'))
- far_field: float32 [512, 128], P('grp')
Inputs may be any that keep to these rules, and one draw needn't show every extreme that they name: `face_partner`: for slot s of a partition, the slot it meets in the coding of the exterior-trace step; slots below 2048 are paired both ways within the partition or meet themselves (the conducting skin); every live entry of a neighbour's list is met by exactly one slot. `send_faces`: each partition's 128 entries of a row list distinct slots, live ones first and -1 after; the upper list of partition p and the lower list of p + 1 have equal live counts, and some pair has all 128 live; partition 0 has no live lower entries and the last none upper. `huy_slots`: the 32 slots of a partition are distinct. `huy_worker`: among the 32 faces of one partition at most 8 name the same worker, and some partition names a worker exactly 8 times.
All inputs are finite; a program needn't handle non-finite values.
Results may differ from a plain program's by a relative error of at most 0.0003.
Values sent between devices are 32-bit elements; how exact they have to be, the bound alone decides.
No kernel may reach another device: no remote copies, remote signals or barrier semaphores. Data moves between devices by JAX's collectives and lax.ppermute only.
A program may use at most 64 MiB of HBM per device.

v0:
```python
import math

import jax
import jax.numpy as jnp
import numpy as np
from jax import lax
from jax.sharding import PartitionSpec as P

CAP = 8
DIRS = 512


rk_alpha = -0.4178904745
rk_beta = 0.3792103129
time_step = 0.5
freq_block = 8
highest = lax.Precision.HIGHEST


def with_halo(cells, sides, width):
    for axis, dim in sides:
        count = lax.axis_size(axis)
        ends = count - 1
        head = lax.slice_in_dim(cells, 0, width, axis=dim)
        tail = lax.slice_in_dim(cells, cells.shape[dim] - width, cells.shape[dim], axis=dim)
        cells = jnp.concatenate(
            [
                lax.ppermute(tail, axis, [(i, (i + 1) % count) for i in range(ends)]),
                cells,
                lax.ppermute(head, axis, [((i + 1) % count, i) for i in range(ends)]),
            ],
            axis=dim,
        )
    return cells


def face_nodes():
    lattice = [
        (along_a, along_b, along_c)
        for along_c in range(4)
        for along_b in range(4 - along_c)
        for along_a in range(4 - along_b - along_c)
    ]
    checkers = [
        lambda point_abc: point_abc[2] == 0,
        lambda point_abc: point_abc[1] == 0,
        lambda point_abc: sum(point_abc) == 3,
        lambda point_abc: point_abc[0] == 0,
    ]
    face_rows = []
    for checker in checkers:
        face_rows.append(
            [node_id for node_id, point_abc in enumerate(lattice) if checker(point_abc)]
        )
    return np.array(face_rows, dtype=np.int32)


def face_traces(values):
    node_table = face_nodes()
    elements = values.shape[2]
    picked = values[:, node_table.reshape(-1), :]
    picked = picked.reshape(values.shape[0], 4, node_table.shape[1], elements)
    return picked.transpose(0, 2, 1, 3).reshape(values.shape[0], node_table.shape[1], 4 * elements)


def cross_product(first_vec, second_vec):
    return jnp.stack(
        [
            first_vec[1] * second_vec[2] - first_vec[2] * second_vec[1],
            first_vec[2] * second_vec[0] - first_vec[0] * second_vec[2],
            first_vec[0] * second_vec[1] - first_vec[1] * second_vec[0],
        ]
    )


def section_update(
    fields,
    section_res,
    derivative,
    geometry,
    normals,
    face_scale,
    lift_matrix,
    interp_q,
    project_q,
    mat_table,
    materials,
    profile,
    partner,
    from_below,
    from_above,
):
    elements = fields.shape[2]
    slot_count = 4 * elements
    face_nodes_count = lift_matrix.shape[1] // 4
    derivs = jnp.einsum("rij,cje->rcie", derivative, fields, precision=highest)
    metric = geometry.reshape(3, 3, elements)

    def spatial(direction):
        return (
            metric[0, direction] * derivs[0]
            + metric[1, direction] * derivs[1]
            + metric[2, direction] * derivs[2]
        )

    along_x, along_y, along_z = (spatial(0), spatial(1), spatial(2))
    curl_h = jnp.stack([along_y[5] - along_z[4], along_z[3] - along_x[5], along_x[4] - along_y[3]])
    curl_e = jnp.stack([along_y[2] - along_z[1], along_z[0] - along_x[2], along_x[1] - along_y[0]])
    inside = face_traces(fields)
    extended = jnp.concatenate([inside, from_below, from_above], axis=2)
    outside = jnp.take(extended, partner, axis=2)
    on_skin = (partner == jnp.arange(slot_count, dtype=jnp.int32))[None, None, :]
    jump_e = jnp.where(on_skin, -inside[:3], outside[:3]) - inside[:3]
    jump_h = outside[3:] - inside[3:]
    normal = normals.reshape(3, slot_count)[:, None, :]
    normal_e = jnp.sum(normal * jump_e, axis=0)
    normal_h = jnp.sum(normal * jump_h, axis=0)
    half_scale = 0.5 * face_scale.reshape(slot_count)
    flux_e = (cross_product(normal, jump_h) + jump_e - normal_e * normal) * half_scale
    flux_h = (-cross_product(normal, jump_e) + jump_h - normal_h * normal) * half_scale
    flux_all = jnp.concatenate([flux_e, flux_h]).reshape(6, face_nodes_count, 4, elements)
    flux_all = flux_all.transpose(0, 2, 1, 3).reshape(6, 4 * face_nodes_count, elements)
    lifted = jnp.einsum("ik,cke->cie", lift_matrix, flux_all, precision=highest)
    raw_rate = jnp.concatenate([curl_h, -curl_e]) + lifted
    onehot = (
        materials[None, :] == jnp.arange(mat_table.shape[1], dtype=jnp.int32)[:, None]
    ).astype(jnp.float32)
    base_coef = jnp.dot(mat_table, onehot, precision=highest)
    weights = base_coef[:, None, :] * profile
    at_points = jnp.einsum("qj,cje->cqe", interp_q, raw_rate, precision=highest)
    at_points = at_points.reshape(2, 3, interp_q.shape[0], elements) * weights[:, None]
    adjusted = jnp.einsum(
        "jq,cqe->cje",
        project_q,
        at_points.reshape(6, interp_q.shape[0], elements),
        precision=highest,
    )
    new_res = rk_alpha * section_res + time_step * adjusted
    new_fields = fields + rk_beta * new_res
    return (new_fields, new_res)


def huygens_currents(new_fields, normals, huy_slots):
    averaged = jnp.mean(face_traces(new_fields), axis=1)
    picked = jnp.take(averaged, huy_slots, axis=1)
    normal = jnp.take(normals.reshape(3, -1), huy_slots, axis=1)
    return jnp.concatenate([cross_product(normal, picked[3:]), -cross_product(normal, picked[:3])])


def add_spectra(spectra, current, time_phase):
    real_part = jnp.cos(time_phase)[:, None, None] * current[None]
    imag_part = jnp.sin(time_phase)[:, None, None] * current[None]
    return spectra + jnp.concatenate([real_part, imag_part], axis=1)


def far_terms(rows_spec, rows_pos, wavenumber, row_count, norm_scale):
    row_ids = jnp.arange(row_count, dtype=jnp.int32)
    height = 1.0 - (2.0 * row_ids.astype(jnp.float32) + 1.0) / DIRS
    radius = jnp.sqrt(1.0 - height * height)
    azimuth = (row_ids * 381966 % 1000000).astype(jnp.float32) * 1e-06 * (2.0 * math.pi)
    cos_turn = jnp.cos(azimuth)
    sin_turn = jnp.sin(azimuth)
    heading = jnp.stack([radius * cos_turn, radius * sin_turn, height])
    theta_hat = jnp.stack([height * cos_turn, height * sin_turn, -radius])
    phi_hat = jnp.stack([-sin_turn, cos_turn, jnp.zeros_like(cos_turn)])
    path_length = jnp.einsum("xr,xd->rd", rows_pos, heading, precision=highest)
    freq_count = rows_spec.shape[0]
    blocks_spec = rows_spec.reshape(freq_count // freq_block, freq_block, 12, rows_spec.shape[2])
    blocks_wave = wavenumber.reshape(freq_count // freq_block, freq_block)

    def project(summed_vec, unit_vec):
        return (
            unit_vec[0] * summed_vec[:, 0]
            + unit_vec[1] * summed_vec[:, 1]
            + unit_vec[2] * summed_vec[:, 2]
        )

    def components(summed):
        electric = summed[:, :3]
        magnetic = summed[:, 3:]
        return (
            project(electric, theta_hat) + project(magnetic, phi_hat),
            project(magnetic, theta_hat) - project(electric, phi_hat),
        )

    def one_block(block_pair):
        spec_block, wave_block = block_pair
        phase_angle = wave_block[:, None, None] * path_length[None]
        with_cos = jnp.einsum("fcr,frd->fcd", spec_block, jnp.cos(phase_angle), precision=highest)
        with_sin = jnp.einsum("fcr,frd->fcd", spec_block, jnp.sin(phase_angle), precision=highest)
        real_sum = with_cos[:, :6] - with_sin[:, 6:]
        imag_sum = with_sin[:, :6] + with_cos[:, 6:]
        theta_re, phi_re = components(real_sum)
        theta_im, phi_im = components(imag_sum)
        return jnp.stack([theta_re, theta_im, phi_re, phi_im], axis=1)

    result = lax.map(one_block, (blocks_spec, blocks_wave))
    result = (
        result.reshape(freq_count, 4, row_count)
        .transpose(1, 0, 2)
        .reshape(4 * freq_count, row_count)
    )
    return result.T * norm_scale


def per_device(
    fields,
    section_res,
    derivative,
    geometry,
    normals,
    face_scale,
    lift_matrix,
    interp_q,
    project_q,
    mat_table,
    materials,
    profile,
    face_partner,
    send_faces,
    spectra,
    huy_slots,
    huy_worker,
    huy_pos,
    wavenumber,
    time_phase,
):
    shared = send_faces.shape[1]
    inside = face_traces(fields)
    is_live = send_faces >= 0
    picked = jnp.take(inside, jnp.where(is_live, send_faces, 0).reshape(-1), axis=2)
    picked = picked.reshape(6, inside.shape[1], 2, shared).transpose(2, 0, 1, 3)
    outgoing = (picked * is_live[:, None, None, :].astype(jnp.float32)).reshape(
        2, 6 * inside.shape[1], shared
    )
    rim_traces = with_halo(outgoing, ((("dom", "grp"), 0),), 1)
    from_below = rim_traces[0].reshape(6, inside.shape[1], shared)
    from_above = rim_traces[3].reshape(6, inside.shape[1], shared)
    new_fields, new_res = section_update(
        fields,
        section_res,
        derivative,
        geometry,
        normals,
        face_scale,
        lift_matrix,
        interp_q,
        project_q,
        mat_table,
        materials,
        profile,
        face_partner.reshape(-1),
        from_below,
        from_above,
    )
    current = huygens_currents(new_fields, normals, huy_slots)
    new_spectra = add_spectra(spectra, current, time_phase)
    groups = lax.axis_size("grp")
    workers = huy_worker[:, 0]
    onehot = (workers[:, None] == jnp.arange(groups, dtype=jnp.int32)[None, :]).astype(jnp.int32)
    slot_rank = jnp.sum(jnp.cumsum(onehot, axis=0) * onehot, axis=1) - 1
    target = workers * CAP + slot_rank
    placing = (target[:, None] == jnp.arange(groups * CAP, dtype=jnp.int32)[None, :]).astype(
        jnp.float32
    )
    outgoing_spec = jnp.einsum("fch,hs->fcs", new_spectra, placing, precision=highest)
    norm_scale = 1.0 / math.sqrt(huy_slots.shape[0] * lax.axis_size("dom") * groups)
    outgoing_pos = jnp.dot(huy_pos, placing, precision=highest)[None]
    worker_spectra, arrived_pos = (
        lax.all_to_all(outgoing_spec, "grp", split_axis=2, concat_axis=2, tiled=True),
        lax.all_to_all(outgoing_pos, "grp", split_axis=2, concat_axis=2, tiled=True),
    )
    rows_pos = arrived_pos[0]
    dir_share = DIRS // groups
    whole_sum = lax.psum(
        far_terms(worker_spectra, rows_pos, wavenumber, DIRS, norm_scale), ("dom", "grp")
    )
    far_field = lax.dynamic_slice_in_dim(whole_sum, lax.axis_index("grp") * dir_share, dir_share, 0)
    return (new_fields, new_res, new_spectra, worker_spectra, far_field)


def solution(mesh):
    return jax.shard_map(
        per_device,
        mesh=mesh,
        in_specs=(
            P(None, None, ("dom", "grp")),
            P(None, None, ("dom", "grp")),
            P(),
            P(None, ("dom", "grp")),
            P(None, None, ("dom", "grp")),
            P(None, ("dom", "grp")),
            P(),
            P(),
            P(),
            P(),
            P(("dom", "grp")),
            P(None, None, ("dom", "grp")),
            P(None, ("dom", "grp")),
            P(None, ("dom", "grp")),
            P(None, None, ("dom", "grp")),
            P(("dom", "grp")),
            P(("dom", "grp"), None),
            P(None, ("dom", "grp")),
            P(),
            P(),
        ),
        out_specs=(
            P(None, None, ("dom", "grp")),
            P(None, None, ("dom", "grp")),
            P(None, None, ("dom", "grp")),
            P(None, None, ("dom", "grp")),
            P("grp", None),
        ),
        check_vma=False,
    )
```

profile of v0, /device:TPU:1, one launch (start us, length us, event | category | flops | bytes accessed | tf_op | source)
XLA Modules:
  0.0 628.2 jit_solution(5686254940623078610)
XLA Ops:
  9.4 2.5 gather_fusion
  12.2 4.9 copy.283
  17.1 4.1 gather_fusion.1
  22.3 4.0 collective-permute-start
  27.0 4.4 collective-permute-start.1
  31.9 0.7 copy.275
  32.6 5.7 all-to-all-start.1
  39.7 0.9 convolution_bitcast_fusion
  44.8 1.3 reshape.484
  46.2 0.8 reduce.2
  47.3 0.8 reduce.3
  48.4 11.3 %pad_maximum_fusion = f32[6,10,2304]{1,0,2:T(8,128)} fusion(f32[6,10,128]{1,0,2:T(8,128)S(1)} %copy.256, f32[6,10,128]{1,0,2:T(8,128)S(1)} %copy.255, f32[6,10,2048]{1,0,2:T(8,128)} %bitcast.192), kind=kLoop, calls=%fused_computation.53 | loop fusion | flops 276480 | bytes 1105920 | tf_op jit(solution)/shard_map/concatenate | solution.py:110
  59.7 19.4 %gather_fusion.2 = f32[2048,6,10]{2,1,0:T(8,128)} fusion(f32[6,10,2304]{1,0,2:T(8,128)} %pad_maximum_fusion, s32[2048]{0:T(1024)S(1)} %broadcast_clamp_fusion), kind=kCustom, calls=%fused_computation.2 | custom fusion | bytes 991232 | tf_op jit(solution)/shard_map/jit(_take)/gather | solution.py:111
  79.1 5.5 copy.257
  88.3 1.2 multiply_add_fusion
  93.0 1.0 maximum_add_fusion.1
  94.6 0.9 reshape.543
  95.5 6.6 %all-to-all-start = ((f32[8,1,3072]{2,1,0:T(1,128)}), f32[8,1,3072]{2,1,0:T(1,128)S(1)}, u32[]{:S(2)}, u32[]{:S(2)}) async-start(f32[8,1,3072]{2,1,0:T(1,128)} %reshape.543), calls=%async_computation | async-start | bytes 196608 | tf_op jit(solution)/shard_map/all_to_all | solution.py:270
  102.5 7.3 %all-to-all-done = f32[8,1,3072]{2,1,0:T(1,128)S(1)} async-done(((f32[8,1,3072]{2,1,0:T(1,128)}), f32[8,1,3072]{2,1,0:T(1,128)S(1)}, u32[]{:S(2)}, u32[]{:S(2)}) %all-to-all-start) | async-done | bytes 98336 | tf_op jit(solution)/shard_map/all_to_all | solution.py:270
  110.2 0.9 reduce.4
  111.6 40.2 %while.12 = (s32[]{:T(128)}, f32[4,8,4,512]{3,1,2,0:T(8,128)S(1)}, f32[4,8,12,64]{3,2,1,0:T(8,128)S(1)}, f32[4,8]{1,0:T(4,128)}, f32[64,512]{1,0:T(8,128)S(1)}, /*index=5*/s32[]{:T(128)}) while((s32[]{:T(128)}, f32[4,8,4,512]{3,1,2,0:T(8,128)S(1)}, f32[4,8,12,64]{3,2,1,0:T(8,128)S(1)}, f32[4,8]{1,0:T(4,128)}, ...), condition=%wide.region_6.7_spmd.clone.clone, body=%wide.region_5.6_spmd.clone.clone.sunk | while | flops 76329472 | bytes 2587797 | solution.py:197
  112.3 4.3 fusion.109
  116.6 4.3 fusion.111
  122.4 4.3 fusion.109
  126.7 4.3 fusion.111
  132.4 4.3 fusion.109
  136.7 4.3 fusion.111
  142.5 4.3 fusion.109
  146.8 4.3 fusion.111
  152.6 0.9 copy.278
  153.5 466.3 %all-reduce.2.cloned.1.call-done = f32[512,128]{0,1:T(8,128)} async-done(((f32[512,128]{0,1:T(8,128)}), f32[512,128]{0,1:T(8,128)}) %all-reduce.2.cloned.1.call-update) | async-done | bytes 262160 | tf_op jit(solution)/shard_map/psum | solution.py:275
  619.8 0.9 constant_dynamic-slice_fusion.1
  (206 shorter events, 26.3 us)
Async XLA Ops:
  7.2 32.5 %copy-start = (f32[3,20,20]{2,1,0:T(8,128)S(1)}, f32[3,20,20]{2,1,0:T(8,128)}, u32[]{:S(2)}) copy-start(f32[3,20,20]{2,1,0:T(8,128)} %param.30) | copy-start | bytes 14404
  7.2 24.1 %copy-start.21 = (s32[32,1]{0,1:T(1,128)S(1)}, s32[32,1]{0,1:T(1,128)}, u32[]{:S(2)}) copy-start(s32[32,1]{0,1:T(1,128)} %param.44) | copy-start | bytes 388
  7.2 24.5 %copy-start.25 = (f32[3,32]{1,0:T(4,128)S(1)}, f32[3,32]{1,0:T(4,128)}, u32[]{:S(2)}) copy-start(f32[3,32]{1,0:T(4,128)} %param.45) | copy-start | bytes 1156
  7.2 31.3 %copy-start.5 = (f32[3,4,512]{2,1,0:T(4,128)S(1)}, f32[3,4,512]{2,1,0:T(4,128)}, u32[]{:S(2)}) copy-start(f32[3,4,512]{2,1,0:T(4,128)} %param.32) | copy-start | bytes 73732
  9.3 29.6 %copy-start.17 = (s32[1024]{0:T(1024)}, s32[1024]{0:T(1024)S(1)}, u32[]{:S(2)}) copy-start(s32[1024]{0:T(1024)S(1)} %pad_clamp_fusion.2) | copy-start | bytes 12292
  9.3 29.6 %copy-start.28 = (s32[32]{0:T(128)S(1)}, s32[32]{0:T(128)}, u32[]{:S(2)}) copy-start(s32[32]{0:T(128)} %param.43) | copy-start | bytes 388
  9.3 29.7 %copy-start.8 = (s32[4,512]{1,0:T(4,128)S(1)}, s32[4,512]{1,0:T(4,128)}, u32[]{:S(2)}) copy-start(s32[4,512]{1,0:T(4,128)} %param.40) | copy-start | bytes 24580
  9.3 30.4 %copy-start.15 = (f32[4,512]{1,0:T(4,128)S(1)}, f32[4,512]{1,0:T(4,128)}, u32[]{:S(2)}) copy-start(f32[4,512]{1,0:T(4,128)} %param.33) | copy-start | bytes 24580
  9.3 30.4 %copy-start.7 = (f32[9,512]{1,0:T(8,128)S(1)}, f32[9,512]{1,0:T(8,128)}, u32[]{:S(2)}) copy-start(f32[9,512]{1,0:T(8,128)} %param.31) | copy-start | bytes 55300
  9.3 30.4 %copy-start.1 = (f32[6,20,512]{2,1,0:T(8,128)S(1)}, f32[6,20,512]{2,1,0:T(8,128)}, u32[]{:S(2)}) copy-start(f32[6,20,512]{2,1,0:T(8,128)} %param.28) | copy-start | bytes 737284
  9.3 31.3 %copy-start.29 = (f32[32]{0:T(128)S(1)}, f32[32]{0:T(128)}, u32[]{:S(2)}) copy-start(f32[32]{0:T(128)} %param.47) | copy-start | bytes 388
  9.3 32.0 %copy-start.26 = (s32[512]{0:T(512)S(1)}, s32[512]{0:T(512)}, u32[]{:S(2)}) copy-start(s32[512]{0:T(512)} %param.38) | copy-start | bytes 6148
  9.3 32.0 %copy-start.27 = (f32[2,6]{1,0:T(2,128)S(1)}, f32[2,6]{1,0:T(2,128)}, u32[]{:S(2)}) copy-start(f32[2,6]{1,0:T(2,128)} %param.37) | copy-start | bytes 148
  9.3 32.1 %copy-start.6 = (f32[2,23,512]{2,0,1:T(2,128)S(1)}, f32[2,23,512]{2,0,1:T(2,128)}, u32[]{:S(2)}) copy-start(f32[2,23,512]{2,0,1:T(2,128)} %param.39) | copy-start | bytes 282628
  22.3 23.9 %collective-permute-start = (f32[1,60,128]{2,0,1:T(1,128)}, f32[1,60,128]{2,0,1:T(1,128)}, u32[]{:S(2)}, u32[]{:S(2)}) collective-permute-start(f32[1,60,128]{2,0,1:T(1,128)} %bitcast.24), channel_id=1, source_target_pairs={{0,1},{1,2},{2,3},{3,4},{4,5},{5,6},{6,7},{7,8},{8,9},{9,10},{10,1... | collective-permute-start | bytes 92168 | tf_op jit(solution)/shard_map/ppermute | solution.py:28
  27.0 20.3 %collective-permute-start.1 = (f32[1,60,128]{2,0,1:T(1,128)}, f32[1,60,128]{2,0,1:T(1,128)}, u32[]{:S(2)}, u32[]{:S(2)}) collective-permute-start(f32[1,60,128]{2,0,1:T(1,128)} %bitcast.25), channel_id=1, source_target_pairs={{1,0},{2,1},{3,2},{4,3},{5,4},{6,5},{7,6},{8,7},{9,8},{10,9},{11,1... | collective-permute-start | bytes 92168 | tf_op jit(solution)/shard_map/ppermute | solution.py:30
  31.7 9.6 %copy-start.22 = (s32[32]{0:T(128)}, s32[32]{0:T(128)S(1)}, u32[]{:S(2)}) copy-start(s32[32]{0:T(128)S(1)} %fusion.80) | copy-start | bytes 388
  32.6 62.9 %all-to-all-start.1 = ((f32[1,3,64]{1,0,2:T(1,128)}), f32[1,3,64]{1,0,2:T(1,128)S(1)}, u32[]{:S(2)}, u32[]{:S(2)}) async-start(f32[1,3,64]{1,0,2:T(1,128)} %copy.275), calls=%async_computation.1 | async-start | bytes 65536 | tf_op jit(solution)/shard_map/all_to_all | solution.py:271
  38.9 4.1 copy-start.19
  59.7 25.0 %copy-start.14 = (pred[2048]{0:T(1024)(128)(4,1)S(1)}, pred[2048]{0:T(1024)(128)(4,1)}, u32[]{:S(2)}) copy-start(pred[2048]{0:T(1024)(128)(4,1)} %get-tuple-element.297) | copy-start | bytes 6148
  59.7 25.0 %copy-start.13 = (pred[2048]{0:T(1024)(128)(4,1)S(1)}, pred[2048]{0:T(1024)(128)(4,1)}, u32[]{:S(2)}) copy-start(pred[2048]{0:T(1024)(128)(4,1)} %get-tuple-element.296) | copy-start | bytes 6148
  59.7 25.9 %copy-start.16 = (f32[1,4,4,128]{3,1,2,0:T(4,128)S(1)}, f32[1,4,4,128]{3,1,2,0:T(4,128)}, u32[]{:S(2)}) copy-start(f32[1,4,4,128]{3,1,2,0:T(4,128)} %copy.298) | copy-start | bytes 24580
  79.1 8.0 %copy-start.9 = (f32[20,40]{1,0:T(8,128)S(1)}, f32[20,40]{1,0:T(8,128)}, u32[]{:S(2)}) copy-start(f32[20,40]{1,0:T(8,128)} %param.34) | copy-start | bytes 9604
  79.1 8.8 %copy-start.10 = (f32[23,20]{1,0:T(8,128)S(1)}, f32[23,20]{1,0:T(8,128)}, u32[]{:S(2)}) copy-start(f32[23,20]{1,0:T(8,128)} %param.35) | copy-start | bytes 5524
  84.7 6.8 %copy-start.20 = (pred[32]{0:T(512)(128)(4,1)S(1)}, pred[32]{0:T(512)(128)(4,1)}, u32[]{:S(2)}) copy-start(pred[32]{0:T(512)(128)(4,1)} %copy-done.19) | copy-start | bytes 100
  84.7 7.6 %copy-start.24 = (f32[32]{0:T(128)S(1)}, f32[32]{0:T(128)}, u32[]{:S(2)}) copy-start(f32[32]{0:T(128)} %get-tuple-element.302) | copy-start | bytes 388
  85.0 9.1 %copy-start.23 = (s32[32]{0:T(128)S(1)}, s32[32]{0:T(128)}, u32[]{:S(2)}) copy-start(s32[32]{0:T(128)} %copy-done.22) | copy-start | bytes 388
  85.5 16.7 %copy-start.12 = (f32[1,512]{1,0:T(1,128)S(1)}, f32[1,512]{1,0:T(1,128)}, u32[]{:S(2)}) copy-start(f32[1,512]{1,0:T(1,128)} %cosine_multiply_fusion) | copy-start | bytes 6148
  89.5 22.1 %copy-start.2 = (f32[6,20,512]{2,1,0:T(8,128)}, f32[6,20,512]{2,1,0:T(8,128)S(1)}, u32[]{:S(2)}) copy-start(f32[6,20,512]{2,1,0:T(8,128)S(1)} %get-tuple-element.304) | copy-start | bytes 737284
  94.0 17.6 %copy-start.3 = (f32[32,12,32]{2,0,1:T(8,128)}, f32[32,12,32]{2,0,1:T(8,128)S(1)}, u32[]{:S(2)}) copy-start(f32[32,12,32]{2,0,1:T(8,128)S(1)} %maximum_add_fusion.1) | copy-start | bytes 147460
  95.5 14.2 %all-to-all-start = ((f32[8,1,3072]{2,1,0:T(1,128)}), f32[8,1,3072]{2,1,0:T(1,128)S(1)}, u32[]{:S(2)}, u32[]{:S(2)}) async-start(f32[8,1,3072]{2,1,0:T(1,128)} %reshape.543), calls=%async_computation | async-start | bytes 196608 | tf_op jit(solution)/shard_map/all_to_all | solution.py:270
  102.1 517.6 %all-reduce.2.cloned.1.call-start = ((), (), s32[]{:S(2)}) async-start(), calls=%async_computation.2 | async-start | bytes 524288 | tf_op jit(solution)/shard_map/psum | solution.py:275
  (3 other events, 8.3 us)
Sparse Core Ops, SparseCore 0:
  152.7 466.9 all-reduce.1
where the time goes:
time: 629 us; the launch traced here: 628 us
  waiting for transfers between devices  474 us (75%)
  local copies, waits for them, and re-layouts  55.7 us (9%)
  matrix products  38.3 us (6%)
  other arithmetic  24.5 us (4%)
  starting transfers between devices  20.8 us (3%)
  between operations  14.9 us (2%)
    psum x1, waiting for transfers between devices, per_device(): lax.psum(far_terms(worker_spectra, rows_pos, wavenumber, DIRS, norm_scale...  466 us
    gather x2, local copies, waits for them, and re-layouts, section_update(): outside = jnp.take(extended, partner, axis=2)  24.9 us
    dot_general x4, matrix products, one_block(): jnp.einsum('fcr,frd->fcd', spec_block, jnp.sin(phase_angle), precision=hi...  17.3 us
    dot_general x4, matrix products, one_block(): jnp.einsum('fcr,frd->fcd', spec_block, jnp.cos(phase_angle), precision=hi...  17.1 us
  transfers between devices with their start and end apart: 5, of which 2 were waited for; matrix products, arithmetic and copies ran while one was open for 9% of the time, Pallas kernels for 0%

commit v1 on v0

v1 whole, which is shorter than its diff:
```python
import math

import jax
import jax.numpy as jnp
import numpy as np
from jax import lax
from jax.experimental import pallas as pl
from jax.experimental.pallas import tpu as pltpu
from jax.sharding import Mesh
from jax.sharding import PartitionSpec as P

CAP = 8
DIRS = 512
FREQS = 32
ELEMS = 512
HDEV = 32
SHARED = 128
NP = 20
NFP = 10
QPTS = 23
MATS = 6
GRP = 8
GROUPS = 4
CHUNK = 8
MEMBERS = 64
ROWS = CHUNK + 3

rk_alpha = -0.4178904745
rk_beta = 0.3792103129
time_step = 0.5
highest = lax.Precision.HIGHEST
f32 = jnp.float32
bf16 = jnp.bfloat16

COS_POLY = (
    0.9999999891722178,
    -19.73920453207716,
    64.9391189830781,
    -85.4501655363007,
    60.167831622719845,
    -25.968312914489402,
    6.5296098973910475,
)
SIN_POLY = (
    6.283185302554009,
    -41.341700417566,
    81.6051319576367,
    -76.7030251163624,
    42.026002315250366,
    -14.900114558517526,
    3.2384947548003575,
)
ROUNDER = 12582912.0


def face_nodes():
    lattice = [
        (along_a, along_b, along_c)
        for along_c in range(4)
        for along_b in range(4 - along_c)
        for along_a in range(4 - along_b - along_c)
    ]
    checkers = [
        lambda point_abc: point_abc[2] == 0,
        lambda point_abc: point_abc[1] == 0,
        lambda point_abc: sum(point_abc) == 3,
        lambda point_abc: point_abc[0] == 0,
    ]
    return np.array(
        [[n for n, abc in enumerate(lattice) if checker(abc)] for checker in checkers],
        dtype=np.int32,
    )


def constants(dir_order, norm_scale):
    nodes = face_nodes()
    select = np.zeros((64, NP), np.float32)
    on_face = np.zeros((32, 4), np.float32)
    widen = np.zeros((4 * NFP, 192), np.float32)
    for face in range(4):
        for j in range(NFP):
            select[face * 16 + j, nodes[face, j]] = 1.0
            on_face[nodes[face, j], face] = 1.0
            for copy in range(3):
                widen[face * NFP + j, copy * 64 + face * 16 + j] = 1.0
    widen_q = np.zeros((QPTS, 96), np.float32)
    for q in range(QPTS):
        for copy in range(3):
            widen_q[q, copy * 32 + q] = 1.0
    spread = np.zeros((HDEV, 8 * HDEV), np.float32)
    for h in range(HDEV):
        spread[h, h::HDEV] = 1.0
    row_ids = dir_order.astype(np.int64)
    height = 1.0 - (2.0 * row_ids + 1.0) / DIRS
    radius = np.sqrt(1.0 - height * height)
    azimuth = (row_ids * 381966 % 1000000) * 1e-06 * (2.0 * math.pi)
    cos_turn, sin_turn = np.cos(azimuth), np.sin(azimuth)
    zero = np.zeros_like(height)
    directions = np.stack(
        [radius * cos_turn, radius * sin_turn, height]
        + [norm_scale * v for v in (height * cos_turn, height * sin_turn, -radius)]
        + [norm_scale * v for v in (-sin_turn, cos_turn)]
        + [zero] * 8
    ).astype(np.float32)
    return select, on_face, widen, widen_q, spread, directions


def high_low(values):
    high = values.astype(bf16)
    return high, (values - high.astype(f32)).astype(bf16)


def mm(a, b):
    return jnp.dot(a, b, preferred_element_type=f32)


def mm_exact(a, b):
    return jnp.dot(a, b, preferred_element_type=f32, precision=highest)


def one_hot_rows(count, base, row):
    step = min(count, 256)
    ids = lax.broadcasted_iota(jnp.int32, (step, row.shape[1]), 0).astype(f32).astype(bf16)
    pieces = []
    for start in range(base, base + count, step):
        local = row - start
        local = jnp.where((local >= 0) & (local < step), local, -1).astype(f32).astype(bf16)
        pieces.append(jnp.where(ids == local, jnp.ones((), bf16), jnp.zeros((), bf16)))
    return pieces[0] if len(pieces) == 1 else jnp.concatenate(pieces, axis=0)


def cos_sin_turns(turns):
    part = turns - ((turns + ROUNDER) - ROUNDER)
    square = part * part
    cos_part = COS_POLY[-1] * square + COS_POLY[-2]
    sin_part = SIN_POLY[-1] * square + SIN_POLY[-2]
    for c, s in zip(COS_POLY[-3::-1], SIN_POLY[-3::-1]):
        cos_part = cos_part * square + c
        sin_part = sin_part * square + s
    return cos_part, sin_part * part


def column_of(row):
    n = row.shape[1]
    eye = lax.broadcasted_iota(jnp.int32, (n, n), 0) == lax.broadcasted_iota(jnp.int32, (n, n), 1)
    return jnp.sum(jnp.where(eye, row, 0.0), axis=1, keepdims=True)


class Fetched:
    def __init__(self, source, target, sem):
        self.copy = pltpu.make_async_copy(source, target, sem)
        self.target = target
        self.waited = False
        self.copy.start()

    def ref(self):
        if not self.waited:
            self.copy.wait()
            self.waited = True
        return self.target

    def __getitem__(self, key):
        return self.ref()[key]


class Sent:
    def __init__(self, source, target, sem):
        self.source, self.target, self.sem = source, target, sem
        self.copies = []

    def __getitem__(self, key):
        return self.source[key]

    def __setitem__(self, key, value):
        self.source[key] = value

    @property
    def shape(self):
        return self.source.shape

    def send(self, *index):
        source, target = self.source, self.target
        if index:
            source, target = source.at[index], target.at[index]
        sem = self.sem.at[len(self.copies)]
        self.copies.append(pltpu.make_async_copy(source, target, sem))
        self.copies[-1].start()


def moving(kernel, first, fetched, n_in, sent, n_out):
    def wrapped(*refs):
        ins, outs, rest = refs[:n_in], refs[n_in : n_in + n_out], refs[n_in + n_out :]
        targets, sems, rest = rest[:fetched], rest[fetched], rest[fetched + 1 :]
        held = [Fetched(ins[first + i], targets[i], sems.at[i]) for i in range(fetched)]
        going = []
        if sent:
            sources, sems, rest = rest[:sent], rest[sent], rest[sent + 1 :]
            going = [Sent(sources[i], outs[i], sems.at[i]) for i in range(sent)]
        kernel(*ins[:first], *held, *ins[first + fetched :], *going, *outs[sent:], *rest)
        for one in held:
            one.ref()
        for one in going:
            for copy in one.copies:
                copy.wait()

    return wrapped


def call(kernel, name, operands, first, fetched, outs, sent, scratch, limit, micros):
    moved = operands[first : first + fetched]
    scratch_shapes = [pltpu.VMEM(a.shape, a.dtype) for a in moved]
    scratch_shapes.append(pltpu.SemaphoreType.DMA((fetched,)))
    if sent:
        scratch_shapes += [pltpu.VMEM(o.shape, o.dtype) for o in outs[:sent]]
        scratch_shapes.append(pltpu.SemaphoreType.DMA((sent, GROUPS)))
    return pl.pallas_call(
        moving(kernel, first, fetched, len(operands), sent, len(outs)),
        out_shape=tuple(outs),
        in_specs=[SMEM] * first + [HBM] * fetched + [VMEM] * (len(operands) - first - fetched),
        out_specs=tuple([HBM] * sent + [VMEM] * (len(outs) - sent)),
        scratch_shapes=scratch_shapes + scratch,
        cost_estimate=pl.CostEstimate(flops=int(micros * 1e8), bytes_accessed=4 << 20, transcendentals=0),
        compiler_params=pltpu.CompilerParams(vmem_limit_bytes=limit),
        name=name,
    )(*operands)


def trace_kernel(fields_ref, send_ref, select_ref, trace_ref, lower_ref, upper_ref):
    select = select_ref[...].astype(bf16)
    for c in range(6):
        for part, half in enumerate(high_low(fields_ref[c])):
            picked = mm(select, half).astype(bf16)
            for face in range(4):
                trace_ref[part * 96 + c * 16 : part * 96 + (c + 1) * 16, face * ELEMS : (face + 1) * ELEMS] = picked[
                    face * 16 : (face + 1) * 16
                ]
    trace_ref.send()
    send = send_ref[...]
    total = [jnp.zeros((192, SHARED), f32), jnp.zeros((192, SHARED), f32)]
    for face in range(4):
        held = trace_ref[:, face * ELEMS : (face + 1) * ELEMS]
        for row in range(2):
            total[row] = total[row] + mm(held, one_hot_rows(ELEMS, face * ELEMS, send[row : row + 1]))
    lower_ref[...] = total[0][:96] + total[0][96:]
    upper_ref[...] = total[1][:96] + total[1][96:]


def early_kernel(
    wave_ref,
    table_ref,
    fields_ref,
    partner_ref,
    derivative_ref,
    geometry_ref,
    normals_ref,
    interp_ref,
    project_ref,
    lift_ref,
    materials_ref,
    profile_ref,
    slots_ref,
    pos_ref,
    widen_ref,
    widen_q_ref,
    dirs_ref,
    trace_ref,
    phase_ref,
    jump_ref,
    curl_ref,
    weight_ref,
    lift_out_ref,
    project_out_ref,
    normal_out_ref,
    pad_ref,
    grad_ref,
):
    heading = dirs_ref[...]
    pos = pos_ref[...]
    path = jnp.zeros((HDEV, DIRS), f32)
    for k in range(3):
        path = path + column_of(pos[k : k + 1]) * heading[k : k + 1]
    for f in range(FREQS):
        cos_part, sin_part = cos_sin_turns(path * (wave_ref[f] * (0.5 / math.pi)))
        rows = slice((f % 8) * HDEV, (f % 8 + 1) * HDEV)
        for place, half in enumerate(high_low(cos_part) + high_low(sin_part)):
            phase_ref[f // 8, place, rows, :] = half
        if f % 8 == 7:
            phase_ref.send(f // 8)

    slots = slots_ref[...]
    pick = one_hot_rows(ELEMS, 0, slots & (ELEMS - 1))
    face_id = lax.shift_right_logical(slots, 9)
    match = lax.broadcasted_iota(jnp.int32, (4, HDEV), 0) == face_id
    normal_out_ref[...] = jnp.zeros((8, HDEV), f32)
    for k in range(3):
        high, low = high_low(normals_ref[k])
        normal_out_ref[k : k + 1, :] = jnp.sum(
            jnp.where(match, mm(high, pick) + mm(low, pick), 0.0), axis=0, keepdims=True
        )
    normal_out_ref.send()

    interp = interp_ref[...]
    pad_ref[...] = jnp.zeros((96, NP), f32)
    for r in range(3):
        pad_ref[r * 32 : r * 32 + QPTS, :] = mm_exact(interp, derivative_ref[r])
    slope_high, slope_low = high_low(pad_ref[...])
    for c in range(6):
        high, low = high_low(fields_ref[c])
        grad_ref[c] = mm(slope_high, high) + (mm(slope_low, high) + mm(slope_high, low))

    def along(k, c):
        return (
            geometry_ref[k : k + 1, :] * grad_ref[c, 0:32, :]
            + geometry_ref[3 + k : 4 + k, :] * grad_ref[c, 32:64, :]
            + geometry_ref[6 + k : 7 + k, :] * grad_ref[c, 64:96, :]
        )

    curl_ref[0] = along(1, 5) - along(2, 4)
    curl_ref[1] = along(2, 3) - along(0, 5)
    curl_ref[2] = along(0, 4) - along(1, 3)
    curl_ref[3] = along(2, 1) - along(1, 2)
    curl_ref[4] = along(0, 2) - along(2, 0)
    curl_ref[5] = along(1, 0) - along(0, 1)

    material = materials_ref[...]
    for m in range(2):
        base = jnp.zeros((1, ELEMS), f32)
        for k in range(MATS):
            base = jnp.where(material == k, table_ref[m, k], base)
        weight_ref[m] = jnp.zeros((32, ELEMS), f32)
        weight_ref[m, 0:QPTS, :] = profile_ref[:, m, :] * base
    curl_ref.send()
    weight_ref.send()

    pad_ref[0:32, :] = jnp.zeros((32, NP), f32)
    pad_ref[0:QPTS, :] = interp
    lifted = mm_exact(pad_ref[0:32, :], mm_exact(lift_ref[...], widen_ref[...]))
    high, low = high_low(lifted)
    column = lax.broadcasted_iota(jnp.int32, (32, 192), 1)
    lift_out_ref[...] = jnp.where(column < 128, high.astype(f32), low.astype(f32)).astype(bf16)
    projected = mm_exact(project_ref[...], widen_q_ref[...])
    high, low = high_low(projected)
    column = lax.broadcasted_iota(jnp.int32, (NP, 96), 1)
    project_out_ref[...] = jnp.where(column < 64, high.astype(f32), low.astype(f32)).astype(bf16)
    lift_out_ref.send()
    project_out_ref.send()

    for face in range(4):
        lanes = slice(face * ELEMS, (face + 1) * ELEMS)
        mate = partner_ref[face : face + 1, :]
        total = jnp.zeros((192, ELEMS), f32)
        for source in range(4):
            held = trace_ref[:, source * ELEMS : (source + 1) * ELEMS]
            total = total + mm(held, one_hot_rows(ELEMS, source * ELEMS, mate))
        outside = total[:96] + total[96:]
        own = trace_ref[:, lanes].astype(f32)
        inside = own[:96] + own[96:]
        skin = mate == lax.broadcasted_iota(jnp.int32, (1, ELEMS), 1) + face * ELEMS
        jump_ref[:48, lanes] = jnp.where(skin, -inside[:48], outside[:48]) - inside[:48]
        jump_ref[48:, lanes] = outside[48:] - inside[48:]
    jump_ref.send()


def late_kernel(
    below_ref,
    above_ref,
    partner_ref,
    jump_ref,
    normals_ref,
    scale_ref,
    curl_ref,
    weight_ref,
    lift_ref,
    project_ref,
    normal_pick_ref,
    fields_ref,
    res_ref,
    slots_ref,
    workers_ref,
    phase_time_ref,
    on_face_ref,
    spread_ref,
    dirs_ref,
    spectra_ref,
    phase_ref,
    fields_out,
    res_out,
    spectra_out,
    far_out,
    flux_ref,
    points_ref,
    nodal_ref,
    group_ref,
    far_ref,
):
    flux_ref[...] = jnp.zeros(flux_ref.shape, bf16)
    nodal_ref[...] = jnp.zeros(nodal_ref.shape, f32)

    below_high, below_low = high_low(below_ref[...])
    above_high, above_low = high_low(above_ref[...])
    below = jnp.concatenate([below_high, below_low], axis=0)
    above = jnp.concatenate([above_high, above_low], axis=0)
    for face in range(4):
        lanes = slice(face * ELEMS, (face + 1) * ELEMS)
        mate = partner_ref[face : face + 1, :]
        met = mm(below, one_hot_rows(SHARED, 4 * ELEMS, mate)) + mm(
            above, one_hot_rows(SHARED, 4 * ELEMS + SHARED, mate)
        )
        jump = jump_ref[:, lanes] + (met[:96] + met[96:])
        e = [jump[i * 16 : (i + 1) * 16] for i in range(3)]
        h = [jump[i * 16 : (i + 1) * 16] for i in range(3, 6)]
        n = [normals_ref[k, face : face + 1, :] for k in range(3)]
        half = 0.5 * scale_ref[face : face + 1, :]
        normal_e = n[0] * e[0] + n[1] * e[1] + n[2] * e[2]
        normal_h = n[0] * h[0] + n[1] * h[1] + n[2] * h[2]
        for i in range(3):
            a, b = (i + 1) % 3, (i + 2) % 3
            flux_e = (n[a] * h[b] - n[b] * h[a] + e[i] - normal_e * n[i]) * half
            flux_h = (n[b] * e[a] - n[a] * e[b] + h[i] - normal_h * n[i]) * half
            for c, flux in ((i, flux_e), (3 + i, flux_h)):
                high, low = high_low(flux)
                flux_ref[c, face * 16 : (face + 1) * 16, :] = high
                flux_ref[c, 64 + face * 16 : 64 + (face + 1) * 16, :] = low
                flux_ref[c, 128 + face * 16 : 128 + (face + 1) * 16, :] = high

    lift = lift_ref[...]
    project = project_ref[...]
    for c in range(6):
        values = (curl_ref[c] + mm(lift, flux_ref[c])) * weight_ref[c // 3]
        high, low = high_low(values)
        points_ref[c, 0:32, :] = high
        points_ref[c, 32:64, :] = low
        points_ref[c, 64:96, :] = high
        new_res = rk_alpha * res_ref[c] + time_step * mm(project, points_ref[c])
        res_out[c] = new_res
        new_fields = fields_ref[c] + rk_beta * new_res
        fields_out[c] = new_fields
        nodal_ref[c * 32 : c * 32 + NP, :] = new_fields
    fields_out.send()
    res_out.send()

    slots = slots_ref[...]
    pick = one_hot_rows(ELEMS, 0, slots & (ELEMS - 1))
    face_id = lax.shift_right_logical(slots, 9)
    high, low = high_low(nodal_ref[...])
    picked = mm(high, pick) + mm(low, pick)
    on_face = on_face_ref[...]
    mask = jnp.zeros((32, HDEV), f32)
    for face in range(4):
        mask = jnp.where(face_id == face, on_face[:, face : face + 1], mask)
    mean = [
        jnp.sum(picked[c * 32 : (c + 1) * 32] * mask, axis=0, keepdims=True) * (1.0 / NFP)
        for c in range(6)
    ]
    n = [normal_pick_ref[k : k + 1, :] for k in range(3)]
    electric, magnetic = mean[:3], mean[3:]
    current = []
    for sign, field in ((1.0, magnetic), (-1.0, electric)):
        for i in range(3):
            a, b = (i + 1) % 3, (i + 2) % 3
            current.append((n[a] * field[b] - n[b] * field[a]) * sign)

    cos_time, sin_time = cos_sin_turns(phase_time_ref[...] * (0.5 / math.pi))
    turn = (column_of(cos_time), column_of(sin_time))
    for i in range(12):
        updated = spectra_ref[i] + turn[i // 6] * current[i % 6]
        spectra_out[i] = updated
        for g in range(GROUPS):
            group_ref[g, i * 8 : (i + 1) * 8, :] = updated[g * 8 : (g + 1) * 8]

    spectra_out.send()

    workers = workers_ref[...].astype(f32)
    same = column_of(workers) == workers
    earlier = lax.broadcasted_iota(jnp.int32, (HDEV, HDEV), 0) < lax.broadcasted_iota(
        jnp.int32, (HDEV, HDEV), 1
    )
    rank = jnp.sum(jnp.where(same & earlier, 1.0, 0.0), axis=0, keepdims=True)
    target = (rank * GRP + workers).astype(jnp.int32)
    placing = one_hot_rows(GRP * CAP, 0, target)
    nt = (((1,), (1,)), ((), ()))
    high, low = high_low(spectra_out[...].reshape(12 * FREQS, HDEV))
    placed = lax.dot_general(placing, high, nt, preferred_element_type=f32) + lax.dot_general(
        placing, low, nt, preferred_element_type=f32
    )
    for j in range(3):
        far_out[pl.ds(CHUNK + j, MEMBERS, stride=ROWS), :] = placed[:, j * 128 : (j + 1) * 128]

    spread = spread_ref[...].astype(bf16)
    own = (lax.broadcasted_iota(jnp.int32, (192, 256), 0) & 7) == lax.shift_right_logical(
        lax.broadcasted_iota(jnp.int32, (192, 256), 1), 5
    )
    theta = [dirs_ref[3 + k : 4 + k, :] for k in range(3)]
    phi = [dirs_ref[6 + k : 7 + k, :] for k in range(2)]

    def onto_theta(v):
        return theta[0] * v[0] + theta[1] * v[1] + theta[2] * v[2]

    def onto_phi(v):
        return phi[0] * v[0] + phi[1] * v[1]

    for g in range(GROUPS):
        high, low = high_low(group_ref[g])
        rows = jnp.where(own, mm(jnp.concatenate([high, low], axis=0), spread), 0.0).astype(bf16)
        cos_sum = mm(rows, phase_ref[g, 0])
        cos_sum = cos_sum[:96] + (cos_sum[96:] + mm(rows[:96], phase_ref[g, 1]))
        sin_sum = mm(rows, phase_ref[g, 2])
        sin_sum = sin_sum[:96] + (sin_sum[96:] + mm(rows[:96], phase_ref[g, 3]))

        def at(values, i):
            return values[i * 8 : (i + 1) * 8]

        real = [at(cos_sum, i) - at(sin_sum, i + 6) for i in range(6)]
        imag = [at(sin_sum, i) + at(cos_sum, i + 6) for i in range(6)]
        parts = (
            onto_theta(real[:3]) + onto_phi(real[3:]),
            onto_theta(imag[:3]) + onto_phi(imag[3:]),
            onto_theta(real[3:]) - onto_phi(real[:3]),
            onto_theta(imag[3:]) - onto_phi(imag[:3]),
        )
        for c, part in enumerate(parts):
            far_ref[c * FREQS + g * 8 : c * FREQS + (g + 1) * 8, :] = part
    far = far_ref[...].T
    for r in range(CHUNK):
        far_out[pl.ds(r, MEMBERS, stride=ROWS), :] = far[r * MEMBERS : (r + 1) * MEMBERS]


def sum_kernel(arrived_ref, sum_ref, pieces_ref):
    rows = [
        jnp.sum(arrived_ref[pl.ds(r, MEMBERS, stride=ROWS), :], axis=0, keepdims=True) for r in range(CHUNK)
    ]
    total = jnp.concatenate(rows, axis=0)
    for z in range(sum_ref.shape[0]):
        sum_ref[z] = total
    for j in range(3):
        piece = arrived_ref[pl.ds(CHUNK + j, MEMBERS, stride=ROWS), :]
        pieces_ref[:, j] = piece.reshape(MEMBERS // GRP, GRP, 128)


def join_kernel(arrived_ref, pieces_ref, message_ref):
    total = jnp.sum(arrived_ref[...], axis=0)
    for p in range(message_ref.shape[0]):
        message_ref[p, 0] = total
        message_ref[p, 1:] = pieces_ref[p]


def final_kernel(arrived_ref, far_ref, worker_ref, rows_ref):
    for p in range(arrived_ref.shape[0]):
        far_ref[p * CHUNK : (p + 1) * CHUNK, :] = arrived_ref[p, 0]
        for j in range(3):
            rows_ref[j, pl.ds(p, GRP, stride=CAP), :] = arrived_ref[p, 1 + j]
    for j in range(3):
        worker_ref[4 * j : 4 * j + 4] = rows_ref[j].T.reshape(4, FREQS, GRP * CAP)


def sds(shape, dtype=f32):
    return jax.ShapeDtypeStruct(shape, dtype)


VMEM = pl.BlockSpec(memory_space=pltpu.VMEM)
SMEM = pl.BlockSpec(memory_space=pltpu.SMEM)
HBM = pl.BlockSpec(memory_space=pltpu.HBM)
WHOLE = 67043328


def factors(dom):
    return (dom // 8, 4, 2)


def per_device(
    fields,
    section_res,
    derivative,
    geometry,
    normals,
    face_scale,
    lift_matrix,
    interp_q,
    project_q,
    mat_table,
    materials,
    profile,
    face_partner,
    send_faces,
    spectra,
    huy_slots,
    huy_worker,
    huy_pos,
    wavenumber,
    time_phase,
    sizes,
):
    along_z, along_x, cores = sizes
    partitions = along_z * along_x * cores * GRP
    order = np.arange(DIRS).reshape(GRP, MEMBERS // GRP, CHUNK).transpose(2, 1, 0).reshape(-1)
    select, on_face, widen, widen_q, spread, directions = constants(
        order, 1.0 / math.sqrt(HDEV * partitions)
    )
    slots_row = huy_slots.reshape(1, HDEV)

    traces, lower, upper = call(
        trace_kernel,
        "traces",
        (fields, send_faces, select),
        0,
        3,
        (sds((192, 4 * ELEMS), bf16), sds((96, SHARED)), sds((96, SHARED))),
        1,
        [],
        WHOLE,
        2,
    )

    ring = ("z", "x", "core", "y")
    from_below = lax.ppermute(upper, ring, [(i, i + 1) for i in range(partitions - 1)])
    from_above = lax.ppermute(lower, ring, [(i + 1, i) for i in range(partitions - 1)])

    phases, jump, curl, weight, lift3, project3, normal_pick = call(
        early_kernel,
        "early",
        (
            wavenumber,
            mat_table,
            fields,
            face_partner,
            derivative,
            geometry,
            normals,
            interp_q,
            project_q,
            lift_matrix,
            materials.reshape(1, ELEMS),
            profile.transpose(1, 0, 2),
            slots_row,
            huy_pos,
            widen,
            widen_q,
            directions,
            traces,
        ),
        2,
        16,
        (
            sds((GROUPS, 4, 8 * HDEV, DIRS), bf16),
            sds((96, 4 * ELEMS)),
            sds((6, 32, ELEMS)),
            sds((2, 32, ELEMS)),
            sds((32, 192), bf16),
            sds((NP, 96), bf16),
            sds((8, HDEV)),
        ),
        7,
        [pltpu.VMEM((96, NP), f32), pltpu.VMEM((6, 96, ELEMS), f32)],
        WHOLE,
        10,
    )

    new_fields, new_res, spectra_t, message = call(
        late_kernel,
        "late",
        (
            from_below,
            from_above,
            face_partner,
            jump,
            normals,
            face_scale,
            curl,
            weight,
            lift3,
            project3,
            normal_pick,
            fields,
            section_res,
            slots_row,
            huy_worker.reshape(1, HDEV),
            time_phase.reshape(1, FREQS),
            on_face,
            spread,
            directions,
            spectra.transpose(1, 0, 2),
            phases,
        ),
        0,
        21,
        (
            sds((6, NP, ELEMS)),
            sds((6, NP, ELEMS)),
            sds((12, FREQS, HDEV)),
            sds((MEMBERS * ROWS, 4 * FREQS)),
        ),
        3,
        [
            pltpu.VMEM((6, 192, ELEMS), bf16),
            pltpu.VMEM((6, 96, ELEMS), bf16),
            pltpu.VMEM((192, ELEMS), f32),
            pltpu.VMEM((GROUPS, 96, HDEV), f32),
            pltpu.VMEM((4 * FREQS, DIRS), f32),
        ],
        WHOLE,
        8,
    )
    new_spectra = spectra_t.transpose(1, 0, 2)

    chunks = MEMBERS // GRP
    small = dict(compiler_params=pltpu.CompilerParams(vmem_limit_bytes=8 << 20))
    arrived = lax.all_to_all(
        message.reshape(MEMBERS, 1, ROWS * 128), ("x", "core", "y"), 0, 0, tiled=True
    ).reshape(MEMBERS * ROWS, 128)
    part, pieces = pl.pallas_call(
        sum_kernel,
        out_shape=(sds((along_z, CHUNK, 128)), sds((chunks, 3, GRP, 128))),
        in_specs=[VMEM],
        out_specs=(VMEM, VMEM),
        name="sum",
        **small,
    )(arrived)
    part = lax.all_to_all(part, "z", 0, 0, tiled=True)
    message = pl.pallas_call(
        join_kernel,
        out_shape=sds((chunks, 4, CHUNK, 128)),
        in_specs=[VMEM, VMEM],
        out_specs=VMEM,
        name="join",
        **small,
    )(part, pieces)
    arrived = lax.all_to_all(message, ("x", "core"), 0, 0, tiled=True)
    far_field, worker_t = pl.pallas_call(
        final_kernel,
        out_shape=(sds((chunks * CHUNK, 128)), sds((12, FREQS, GRP * CAP))),
        in_specs=[VMEM],
        out_specs=(VMEM, VMEM),
        scratch_shapes=[pltpu.VMEM((3, GRP * CAP, 128), f32)],
        name="final",
        **small,
    )(arrived)
    worker_spectra = worker_t.transpose(1, 0, 2)
    return (new_fields, new_res, new_spectra, worker_spectra, far_field)


def solution(mesh):
    dom = mesh.shape["dom"]
    sizes = factors(dom)
    fine = Mesh(mesh.devices.reshape(*sizes, GRP), ("z", "x", "core", "y"))
    every = ("z", "x", "core", "y")
    last = {1: P(every), 2: P(None, every), 3: P(None, None, every)}
    return jax.shard_map(
        lambda *args: per_device(*args, sizes=sizes),
        mesh=fine,
        in_specs=(
            last[3],
            last[3],
            P(),
            last[2],
            last[3],
            last[2],
            P(),
            P(),
            P(),
            P(),
            last[1],
            last[3],
            last[2],
            last[2],
            last[3],
            last[1],
            P(every, None),
            last[2],
            P(),
            P(),
        ),
        out_specs=(last[3], last[3], last[3], last[3], P("y", None)),
        check_vma=False,
    )
```

time: 629 us -> 89.8 us (0.14)
  waiting for transfers between devices: 474 us -> 0.01 us
  blocking collectives: 0 us -> 60.5 us
  local copies, waits for them, and re-layouts: 55.7 us -> 0 us
  matrix products: 38.3 us -> 0 us
  other arithmetic: 24.5 us -> 0 us
  Pallas kernels: 0 us -> 19.9 us
  between operations: 14.9 us -> 0.69 us
  starting transfers between devices: 20.8 us -> 8.4 us
    psum x1 -> x0, waiting for transfers between devices: 466 us -> none  [per_device(): lax.psum(far_terms(worker_spectra, rows_pos, wavenumber, DIRS, norm_scale...]
    all_to_all x0 -> x3, blocking collectives: none -> 60.5 us  [the longest x1 24.4 us: per_device(): part = lax.all_to_all(part, 'z', 0, 0, tiled=True)]
    dot_general x16 -> x0, matrix products: 38.3 us -> none  [the longest x4 17.3 us: one_block(): jnp.einsum('fcr,frd->fcd', spec_block, jnp.sin(phase_angle), precision=hi...]
    gather x9 -> x0, local copies, waits for them, and re-layouts: 34.2 us -> none  [the longest x2 24.9 us: section_update(): outside = jnp.take(extended, partner, axis=2)]
    pallas_call x0 -> x6, Pallas kernels: none -> 19.9 us  [the longest x3 19 us: call(): pl.pallas_call(moving(kernel, first, fetched, len(operands), sent, len(ou...]
    all_to_all x2 -> x0, starting transfers between devices: 12.4 us -> none  [the longest x1 6.65 us: per_device(): lax.all_to_all(outgoing_spec, 'grp', split_axis=2, concat_axis=2, tiled=T...]
    concatenate x3 -> x0, other arithmetic: 11.4 us -> none  [the longest x1 11.3 us: section_update(): extended = jnp.concatenate([inside, from_below, from_above], axis=2)]
    all_to_all x2 -> x0, waiting for transfers between devices: 7.28 us -> none  [the longest x1 7.28 us: per_device(): lax.all_to_all(outgoing_spec, 'grp', split_axis=2, concat_axis=2, tiled=T...]
  transfers between devices with their start and end apart: 5 -> 2, of which waited for: 2 -> 0; matrix products, arithmetic and copies ran while one was open for 9% -> 0% of each run, Pallas kernels for 0% -> 11%
where the time goes in v1:
time: 89.8 us; the launch traced here: 89.5 us
  blocking collectives  60.5 us (67%)
  Pallas kernels  19.9 us (22%)
  starting transfers between devices  8.4 us (9%)
    all_to_all x1, blocking collectives, per_device(): part = lax.all_to_all(part, 'z', 0, 0, tiled=True)  24.4 us
    all_to_all x1, blocking collectives, per_device(): lax.all_to_all(message.reshape(MEMBERS, 1, ROWS * 128), ('x', 'core', 'y'...  24.2 us
    pallas_call x3, Pallas kernels, call(): pl.pallas_call(moving(kernel, first, fetched, len(operands), sent, len(ou...  19 us
    all_to_all x1, blocking collectives, per_device(): arrived = lax.all_to_all(message, ('x', 'core'), 0, 0, tiled=True)  11.9 us
    ppermute x1, starting transfers between devices, per_device(): lax.ppermute(lower, ring, [(i + 1, i) for i in range(partitions - 1)])  4.38 us
    ppermute x1, starting transfers between devices, per_device(): lax.ppermute(upper, ring, [(i, i + 1) for i in range(partitions - 1)])  4.03 us
  transfers between devices with their start and end apart: 2, of which 0 were waited for; matrix products, arithmetic and copies ran while one was open for 0% of the time, Pallas kernels for 11%

profile of v1, /device:TPU:1, one launch (start us, length us, event | category | flops | bytes accessed | tf_op | source)
XLA Modules:
  0.0 89.5 jit_solution(4621396460784621599)
XLA Ops:
  0.6 2.9 %traces.1 = (bf16[192,2048]{1,0:T(8,128)(2,1)}, f32[96,128]{1,0:T(8,128)}, f32[96,128]{1,0:T(8,128)}) custom-call(f32[6,20,512]{2,1,0:T(8,128)} %refs_11_.1, s32[2,128]{1,0:T(2,128)} %refs_1_.2, f32[64,20]{1,0:T(8,128)} %constant.12.clone.refs_2_), custom_call_target="tpu_custom_call" | custom-call | flops 200000000 | bytes 4194304 | tf_op jit(solution)/shard_map/traces/pallas_call | solution.py:216
  3.5 4.0 %collective-permute-start = (f32[96,128]{1,0:T(8,128)}, f32[96,128]{1,0:T(8,128)}, u32[]{:S(2)}, u32[]{:S(2)}) collective-permute-start(f32[96,128]{1,0:T(8,128)} %get-tuple-element.23), channel_id=1, source_target_pairs={{0,1},{1,2},{2,3},{3,4},{4,5},{5,6},{6,7},{7,8},{8,9},{9,10},{10,1... | collective-permute-start | bytes 147464 | tf_op jit(solution)/shard_map/ppermute | solution.py:615
  7.6 4.4 %collective-permute-start.1 = (f32[96,128]{1,0:T(8,128)}, f32[96,128]{1,0:T(8,128)}, u32[]{:S(2)}, u32[]{:S(2)}) collective-permute-start(f32[96,128]{1,0:T(8,128)} %get-tuple-element.24), channel_id=1, source_target_pairs={{1,0},{2,1},{3,2},{4,3},{5,4},{6,5},{7,6},{8,7},{9,8},{10,9},{11,1... | collective-permute-start | bytes 147464 | tf_op jit(solution)/shard_map/ppermute | solution.py:616
  12.0 9.5 %early.1 = (bf16[4,4,256,512]{3,2,1,0:T(8,128)(2,1)}, f32[96,2048]{1,0:T(8,128)}, f32[6,32,512]{2,1,0:T(8,128)}, f32[2,32,512]{2,1,0:T(8,128)}, bf16[32,192]{1,0...) custom-call(f32[32]{0:T(128)} %refs_0_.3, f32[2,6]{1,0:T(2,128)} %refs_1_.3, f32[6,20,512]{2,1,0:T(8,128)} %refs_11_.1, ...), custom_call_target="tpu_custom_call" | custom-call | flops 1000000000 | bytes 4194304 | tf_op jit(solution)/shard_map/early/pallas_call | solution.py:216
  21.5 0.0 collective-permute-done.refs_0_
  21.5 0.0 collective-permute-done.1.refs_1_
  21.5 6.6 %late.1 = (f32[6,20,512]{2,1,0:T(8,128)}, f32[6,20,512]{2,1,0:T(8,128)}, f32[12,32,32]{2,1,0:T(8,128)}, f32[704,128]{1,0:T(8,128)}) custom-call(f32[96,128]{1,0:T(8,128)} %collective-permute-done.refs_0_, f32[96,128]{1,0:T(8,128)} %collective-permute-done.1.refs_1_, s32[4,512]{1,0:T(4,128)} %refs_2_.4, f32[96,2048]{1,0:T(8,128)} %get-tuple-element.26.refs_3_, ...), custom_call_target="tpu_custom_call" | custom-call | flops 800000000 | bytes 4194304 | tf_op jit(solution)/shard_map/late/pallas_call | solution.py:216
  28.1 24.2 %all_to_all.15 = f32[64,1,1408]{2,1,0:T(1,128)S(1)} all-to-all(f32[64,1,1408]{2,1,0:T(1,128)} %bitcast.11), channel_id=1, replica_groups=mesh['z'=12,'x'=4,'core'=2,'y'=8] {'x','core','y'}, dimensions={0} | all-to-all | bytes 720896 | tf_op jit(solution)/shard_map/all_to_all | solution.py:707
  52.4 24.4 %all_to_all.16.arrived_ref = f32[12,8,128]{2,1,0:T(8,128)S(1)} all-to-all(f32[12,8,128]{2,1,0:T(8,128)S(1)} %get-tuple-element.37), channel_id=1, replica_groups=mesh['z'=12,'x'=4,'core'=2,'y'=8] {'z'}, dimensions={0} | all-to-all | bytes 98304 | tf_op jit(solution)/shard_map/all_to_all | solution.py:718
  76.8 11.9 %all_to_all.17.arrived_ref = f32[8,4,8,128]{3,2,1,0:T(8,128)S(1)} all-to-all(f32[8,4,8,128]{3,2,1,0:T(8,128)S(1)} %join.1), channel_id=1, replica_groups=mesh['z'=12,'x'=4,'core'=2,'y'=8] {'x','core'}, dimensions={0} | all-to-all | bytes 262144 | tf_op jit(solution)/shard_map/all_to_all | solution.py:727
  88.6 0.8 final.1
  (2 shorter events, 0.0 us)
Async XLA Ops:
  3.5 17.9 %collective-permute-start = (f32[96,128]{1,0:T(8,128)}, f32[96,128]{1,0:T(8,128)}, u32[]{:S(2)}, u32[]{:S(2)}) collective-permute-start(f32[96,128]{1,0:T(8,128)} %get-tuple-element.23), channel_id=1, source_target_pairs={{0,1},{1,2},{2,3},{3,4},{4,5},{5,6},{6,7},{7,8},{8,9},{9,10},{10,1... | collective-permute-start | bytes 147464 | tf_op jit(solution)/shard_map/ppermute | solution.py:615
  7.6 13.9 %collective-permute-start.1 = (f32[96,128]{1,0:T(8,128)}, f32[96,128]{1,0:T(8,128)}, u32[]{:S(2)}, u32[]{:S(2)}) collective-permute-start(f32[96,128]{1,0:T(8,128)} %get-tuple-element.24), channel_id=1, source_target_pairs={{1,0},{2,1},{3,2},{4,3},{5,4},{6,5},{7,6},{8,7},{9,8},{10,9},{11,1... | collective-permute-start | bytes 147464 | tf_op jit(solution)/shard_map/ppermute | solution.py:616

commit v2 on v1

--- a/solution.py
+++ b/solution.py
@@ -33,22 +33,18 @@
 bf16 = jnp.bfloat16
 
 COS_POLY = (
-    0.9999999891722178,
-    -19.73920453207716,
-    64.9391189830781,
-    -85.4501655363007,
-    60.167831622719845,
-    -25.968312914489402,
-    6.5296098973910475,
+    1.4142134965648603,
+    -6.97885098821926,
+    5.73946117028719,
+    -1.8835629847749262,
+    0.3106981867542991,
 )
 SIN_POLY = (
-    6.283185302554009,
-    -41.341700417566,
-    81.6051319576367,
-    -76.7030251163624,
-    42.026002315250366,
-    -14.900114558517526,
-    3.2384947548003575,
+    4.442882919199669,
+    -7.308245696155,
+    3.606354411402601,
+    -0.8461128855994527,
+    0.10982698719081677,
 )
 ROUNDER = 12582912.0
 
@@ -74,12 +70,10 @@
 
 def constants(dir_order, norm_scale):
     nodes = face_nodes()
-    select = np.zeros((64, NP), np.float32)
     on_face = np.zeros((32, 4), np.float32)
     widen = np.zeros((4 * NFP, 192), np.float32)
     for face in range(4):
         for j in range(NFP):
-            select[face * 16 + j, nodes[face, j]] = 1.0
             on_face[nodes[face, j], face] = 1.0
             for copy in range(3):
                 widen[face * NFP + j, copy * 64 + face * 16 + j] = 1.0
@@ -102,7 +96,7 @@
         + [norm_scale * v for v in (-sin_turn, cos_turn)]
         + [zero] * 8
     ).astype(np.float32)
-    return select, on_face, widen, widen_q, spread, directions
+    return on_face, widen, widen_q, spread, directions
 
 
 def high_low(values):
@@ -132,12 +126,13 @@
 def cos_sin_turns(turns):
     part = turns - ((turns + ROUNDER) - ROUNDER)
     square = part * part
-    cos_part = COS_POLY[-1] * square + COS_POLY[-2]
-    sin_part = SIN_POLY[-1] * square + SIN_POLY[-2]
+    cos_half = COS_POLY[-1] * square + COS_POLY[-2]
+    sin_half = SIN_POLY[-1] * square + SIN_POLY[-2]
     for c, s in zip(COS_POLY[-3::-1], SIN_POLY[-3::-1]):
-        cos_part = cos_part * square + c
-        sin_part = sin_part * square + s
-    return cos_part, sin_part * part
+        cos_half = cos_half * square + c
+        sin_half = sin_half * square + s
+    sin_half = sin_half * part
+    return 1.0 - sin_half * sin_half, sin_half * cos_half
 
 
 def column_of(row):
@@ -190,8 +185,10 @@
 def moving(kernel, first, fetched, n_in, sent, n_out):
     def wrapped(*refs):
         ins, outs, rest = refs[:n_in], refs[n_in : n_in + n_out], refs[n_in + n_out :]
-        targets, sems, rest = rest[:fetched], rest[fetched], rest[fetched + 1 :]
-        held = [Fetched(ins[first + i], targets[i], sems.at[i]) for i in range(fetched)]
+        held = []
+        if fetched:
+            targets, sems, rest = rest[:fetched], rest[fetched], rest[fetched + 1 :]
+            held = [Fetched(ins[first + i], targets[i], sems.at[i]) for i in range(fetched)]
         going = []
         if sent:
             sources, sems, rest = rest[:sent], rest[sent], rest[sent + 1 :]
@@ -209,7 +206,8 @@
 def call(kernel, name, operands, first, fetched, outs, sent, scratch, limit, micros):
     moved = operands[first : first + fetched]
     scratch_shapes = [pltpu.VMEM(a.shape, a.dtype) for a in moved]
-    scratch_shapes.append(pltpu.SemaphoreType.DMA((fetched,)))
+    if fetched:
+        scratch_shapes.append(pltpu.SemaphoreType.DMA((fetched,)))
     if sent:
         scratch_shapes += [pltpu.VMEM(o.shape, o.dtype) for o in outs[:sent]]
         scratch_shapes.append(pltpu.SemaphoreType.DMA((sent, GROUPS)))
@@ -219,14 +217,21 @@
         in_specs=[SMEM] * first + [HBM] * fetched + [VMEM] * (len(operands) - first - fetched),
         out_specs=tuple([HBM] * sent + [VMEM] * (len(outs) - sent)),
         scratch_shapes=scratch_shapes + scratch,
-        cost_estimate=pl.CostEstimate(flops=int(micros * 1e8), bytes_accessed=4 << 20, transcendentals=0),
+        cost_estimate=pl.CostEstimate(flops=int(micros * 1.15e9), bytes_accessed=4 << 20, transcendentals=0),
         compiler_params=pltpu.CompilerParams(vmem_limit_bytes=limit),
         name=name,
     )(*operands)
 
 
-def trace_kernel(fields_ref, send_ref, select_ref, trace_ref, lower_ref, upper_ref):
-    select = select_ref[...].astype(bf16)
+def trace_kernel(fields_ref, send_ref, trace_ref, lower_ref, upper_ref):
+    where = lax.broadcasted_iota(jnp.int32, (64, NP), 0) * 32 + lax.broadcasted_iota(
+        jnp.int32, (64, NP), 1
+    )
+    chosen = jnp.zeros((64, NP), f32)
+    for face, row in enumerate(face_nodes()):
+        for j, node in enumerate(row):
+            chosen = jnp.where(where == (face * 16 + j) * 32 + int(node), 1.0, chosen)
+    select = chosen.astype(bf16)
     for c in range(6):
         for part, half in enumerate(high_low(fields_ref[c])):
             picked = mm(select, half).astype(bf16)
@@ -234,7 +239,6 @@
                 trace_ref[part * 96 + c * 16 : part * 96 + (c + 1) * 16, face * ELEMS : (face + 1) * ELEMS] = picked[
                     face * 16 : (face + 1) * 16
                 ]
-    trace_ref.send()
     send = send_ref[...]
     total = [jnp.zeros((192, SHARED), f32), jnp.zeros((192, SHARED), f32)]
     for face in range(4):
@@ -284,8 +288,6 @@
         rows = slice((f % 8) * HDEV, (f % 8 + 1) * HDEV)
         for place, half in enumerate(high_low(cos_part) + high_low(sin_part)):
             phase_ref[f // 8, place, rows, :] = half
-        if f % 8 == 7:
-            phase_ref.send(f // 8)
 
     slots = slots_ref[...]
     pick = one_hot_rows(ELEMS, 0, slots & (ELEMS - 1))
@@ -297,7 +299,6 @@
         normal_out_ref[k : k + 1, :] = jnp.sum(
             jnp.where(match, mm(high, pick) + mm(low, pick), 0.0), axis=0, keepdims=True
         )
-    normal_out_ref.send()
 
     interp = interp_ref[...]
     pad_ref[...] = jnp.zeros((96, NP), f32)
@@ -329,8 +330,6 @@
             base = jnp.where(material == k, table_ref[m, k], base)
         weight_ref[m] = jnp.zeros((32, ELEMS), f32)
         weight_ref[m, 0:QPTS, :] = profile_ref[:, m, :] * base
-    curl_ref.send()
-    weight_ref.send()
 
     pad_ref[0:32, :] = jnp.zeros((32, NP), f32)
     pad_ref[0:QPTS, :] = interp
@@ -342,8 +341,6 @@
     high, low = high_low(projected)
     column = lax.broadcasted_iota(jnp.int32, (NP, 96), 1)
     project_out_ref[...] = jnp.where(column < 64, high.astype(f32), low.astype(f32)).astype(bf16)
-    lift_out_ref.send()
-    project_out_ref.send()
 
     for face in range(4):
         lanes = slice(face * ELEMS, (face + 1) * ELEMS)
@@ -358,7 +355,6 @@
         skin = mate == lax.broadcasted_iota(jnp.int32, (1, ELEMS), 1) + face * ELEMS
         jump_ref[:48, lanes] = jnp.where(skin, -inside[:48], outside[:48]) - inside[:48]
         jump_ref[48:, lanes] = outside[48:] - inside[48:]
-    jump_ref.send()
 
 
 def late_kernel(
@@ -561,6 +557,7 @@
 SMEM = pl.BlockSpec(memory_space=pltpu.SMEM)
 HBM = pl.BlockSpec(memory_space=pltpu.HBM)
 WHOLE = 67043328
+PART = 36 << 20
 
 
 def factors(dom):
@@ -593,7 +590,7 @@
     along_z, along_x, cores = sizes
     partitions = along_z * along_x * cores * GRP
     order = np.arange(DIRS).reshape(GRP, MEMBERS // GRP, CHUNK).transpose(2, 1, 0).reshape(-1)
-    select, on_face, widen, widen_q, spread, directions = constants(
+    on_face, widen, widen_q, spread, directions = constants(
         order, 1.0 / math.sqrt(HDEV * partitions)
     )
     slots_row = huy_slots.reshape(1, HDEV)
@@ -601,13 +598,13 @@
     traces, lower, upper = call(
         trace_kernel,
         "traces",
-        (fields, send_faces, select),
+        (fields, send_faces),
         0,
-        3,
+        0,
         (sds((192, 4 * ELEMS), bf16), sds((96, SHARED)), sds((96, SHARED))),
-        1,
+        0,
         [],
-        WHOLE,
+        PART,
         2,
     )
 
@@ -639,7 +636,7 @@
             traces,
         ),
         2,
-        16,
+        0,
         (
             sds((GROUPS, 4, 8 * HDEV, DIRS), bf16),
             sds((96, 4 * ELEMS)),
@@ -649,9 +646,9 @@
             sds((NP, 96), bf16),
             sds((8, HDEV)),
         ),
-        7,
+        0,
         [pltpu.VMEM((96, NP), f32), pltpu.VMEM((6, 96, ELEMS), f32)],
-        WHOLE,
+        PART,
         10,
     )
 
@@ -682,7 +679,7 @@
             phases,
         ),
         0,
-        21,
+        0,
         (
             sds((6, NP, ELEMS)),
             sds((6, NP, ELEMS)),
@@ -697,7 +694,7 @@
             pltpu.VMEM((GROUPS, 96, HDEV), f32),
             pltpu.VMEM((4 * FREQS, DIRS), f32),
         ],
-        WHOLE,
+        PART,
         8,
     )
     new_spectra = spectra_t.transpose(1, 0, 2)

time: 89.8 us -> 83.5 us (0.930)
  Pallas kernels: 19.9 us -> 11.7 us
  local copies, waits for them, and re-layouts: 0 us -> 1.75 us
    pallas_call x3, Pallas kernels: 19 us -> 10.8 us  [call(): pl.pallas_call(moving(kernel, first, fetched, len(operands), sent, len(ou...]
    unnamed x0 -> x50, local copies, waits for them, and re-layouts: none -> 1.75 us
  transfers between devices with their start and end apart: 2 -> 2, of which waited for: 0 -> 0; matrix products, arithmetic and copies ran while one was open for 0% -> 0% of each run, Pallas kernels for 11% -> 7%
where the time goes in v2:
time: 83.5 us; the launch traced here: 83.2 us
  blocking collectives  60.3 us (72%)
  Pallas kernels  11.7 us (14%)
  starting transfers between devices  8.41 us (10%)
  local copies, waits for them, and re-layouts  1.75 us (2%)
  between operations  1.04 us (1%)
    all_to_all x1, blocking collectives, per_device(): part = lax.all_to_all(part, 'z', 0, 0, tiled=True)  24.4 us
    all_to_all x1, blocking collectives, per_device(): lax.all_to_all(message.reshape(MEMBERS, 1, ROWS * 128), ('x', 'core', 'y'...  24 us
    all_to_all x1, blocking collectives, per_device(): arrived = lax.all_to_all(message, ('x', 'core'), 0, 0, tiled=True)  11.9 us
    pallas_call x3, Pallas kernels, call(): pl.pallas_call(moving(kernel, first, fetched, len(operands), sent, len(ou...  10.8 us
    ppermute x1, starting transfers between devices, per_device(): lax.ppermute(lower, ring, [(i + 1, i) for i in range(partitions - 1)])  4.37 us
    ppermute x1, starting transfers between devices, per_device(): lax.ppermute(upper, ring, [(i, i + 1) for i in range(partitions - 1)])  4.03 us
    unnamed x50, local copies, waits for them, and re-layouts  1.75 us
  transfers between devices with their start and end apart: 2, of which 0 were waited for; matrix products, arithmetic and copies ran while one was open for 0% of the time, Pallas kernels for 7%

profile of v2, /device:TPU:1, one launch (start us, length us, event | category | flops | bytes accessed | tf_op | source)
XLA Modules:
  0.0 83.2 jit_solution(8970546549775315662)
XLA Ops:
  0.6 0.0 copy-start
  0.6 1.0 %copy-done = f32[6,20,512]{2,1,0:T(8,128)S(1)} copy-done((f32[6,20,512]{2,1,0:T(8,128)S(1)}, f32[6,20,512]{2,1,0:T(8,128)}, u32[]{:S(2)}) %copy-start) | copy-done | bytes 245784
  1.6 0.7 copy-done.14
  2.3 0.0 copy-start.7
  2.4 0.0 copy-start.20
  2.4 0.0 copy-start.21
  2.4 0.0 copy-start.24
  2.4 0.9 %traces.1 = (bf16[192,2048]{1,0:T(8,128)(2,1)S(1)}, f32[96,128]{1,0:T(8,128)S(1)}, f32[96,128]{1,0:T(8,128)S(1)}) custom-call(f32[6,20,512]{2,1,0:T(8,128)S(1)} %copy-done, s32[2,128]{1,0:T(2,128)S(1)} %copy-done.14), custom_call_target="tpu_custom_call" | custom-call | flops 2300000000 | bytes 4194304 | tf_op jit(solution)/shard_map/traces/pallas_call | solution.py:214
  3.3 4.0 %collective-permute-start = (f32[96,128]{1,0:T(8,128)S(1)}, f32[96,128]{1,0:T(8,128)S(1)}, u32[]{:S(2)}, u32[]{:S(2)}) collective-permute-start(f32[96,128]{1,0:T(8,128)S(1)} %get-tuple-element.23), channel_id=1, source_target_pairs={{0,1},{1,2},{2,3},{3,4},{4,5},{5,6},{6,7},{7,8},{8,9},{9,10},{10,1... | collective-permute-start | bytes 147464 | tf_op jit(solution)/shard_map/ppermute | solution.py:612
  7.4 4.4 %collective-permute-start.1 = (f32[96,128]{1,0:T(8,128)S(1)}, f32[96,128]{1,0:T(8,128)S(1)}, u32[]{:S(2)}, u32[]{:S(2)}) collective-permute-start(f32[96,128]{1,0:T(8,128)S(1)} %get-tuple-element.24), channel_id=1, source_target_pairs={{1,0},{2,1},{3,2},{4,3},{5,4},{6,5},{7,6},{8,7},{9,8},{10,9},{11,1... | collective-permute-start | bytes 147464 | tf_op jit(solution)/shard_map/ppermute | solution.py:613
  11.9 0.0 copy-start.1
  11.9 0.0 copy-start.2
  11.9 0.0 copy-start.11
  12.0 0.0 copy-start.18
  12.0 0.0 copy-start.19
  12.0 0.0 copy-start.22
  12.0 0.0 copy-start.23
  12.0 5.5 %early.1 = (bf16[4,4,256,512]{3,2,1,0:T(8,128)(2,1)S(1)}, f32[96,2048]{1,0:T(8,128)S(1)}, f32[6,32,512]{2,1,0:T(8,128)S(1)}, f32[2,32,512]{2,1,0:T(8,128)S(1)}, ...) custom-call(f32[32]{0:T(128)S(1)} %copy-done.16, f32[2,6]{1,0:T(2,128)S(1)} %copy-done.15, ...), custom_call_target="tpu_custom_call" | custom-call | flops 11500000256 | bytes 4194304 | tf_op jit(solution)/shard_map/early/pallas_call | solution.py:214
  17.5 0.0 collective-permute-done.refs_0_
  17.5 0.0 collective-permute-done.1.refs_1_
  17.5 0.0 copy-done.1
  17.5 0.0 copy-done.2
  17.6 0.0 copy-done.11
  17.6 0.0 copy-done.18
  17.6 0.0 copy-done.19
  17.6 0.0 copy-done.22
  17.6 0.0 copy-done.23
  17.6 4.4 %late.1 = (f32[6,20,512]{2,1,0:T(8,128)}, f32[6,20,512]{2,1,0:T(8,128)}, f32[12,32,32]{2,1,0:T(8,128)}, f32[704,128]{1,0:T(8,128)S(1)}) custom-call(f32[96,128]{1,0:T(8,128)S(1)} %collective-permute-done.refs_0_, f32[96,128]{1,0:T(8,128)S(1)} %collective-permute-done.1.refs_1_, s32[4,512]{1,0:T(4,128)S(1)} %copy-done.10, ...), custom_call_target="tpu_custom_call" | custom-call | flops 9200000000 | bytes 4194304 | tf_op jit(solution)/shard_map/late/pallas_call | solution.py:214
  22.0 24.0 %all_to_all.15 = f32[64,1,1408]{2,1,0:T(1,128)S(1)} all-to-all(f32[64,1,1408]{2,1,0:T(1,128)S(1)} %bitcast.11), channel_id=1, replica_groups=mesh['z'=12,'x'=4,'core'=2,'y'=8] {'x','core','y'}, dimensions={0} | all-to-all | bytes 720896 | tf_op jit(solution)/shard_map/all_to_all | solution.py:704
  46.1 24.4 %all_to_all.16.arrived_ref = f32[12,8,128]{2,1,0:T(8,128)S(1)} all-to-all(f32[12,8,128]{2,1,0:T(8,128)S(1)} %get-tuple-element.37), channel_id=1, replica_groups=mesh['z'=12,'x'=4,'core'=2,'y'=8] {'z'}, dimensions={0} | all-to-all | bytes 98304 | tf_op jit(solution)/shard_map/all_to_all | solution.py:715
  70.5 11.9 %all_to_all.17.arrived_ref = f32[8,4,8,128]{3,2,1,0:T(8,128)S(1)} all-to-all(f32[8,4,8,128]{3,2,1,0:T(8,128)S(1)} %join.1), channel_id=1, replica_groups=mesh['z'=12,'x'=4,'core'=2,'y'=8] {'x','core'}, dimensions={0} | all-to-all | bytes 262144 | tf_op jit(solution)/shard_map/all_to_all | solution.py:724
  82.3 0.8 final.1
  (31 shorter events, 0.1 us)
Async XLA Ops:
  0.6 1.0 %copy-start = (f32[6,20,512]{2,1,0:T(8,128)S(1)}, f32[6,20,512]{2,1,0:T(8,128)}, u32[]{:S(2)}) copy-start(f32[6,20,512]{2,1,0:T(8,128)} %refs_11_.1) | copy-start | bytes 737284
  1.6 0.7 copy-start.14
  2.3 9.5 %copy-start.3 = (f32[2,23,512]{2,0,1:T(2,128)S(1)}, f32[2,23,512]{2,0,1:T(2,128)}, u32[]{:S(2)}) copy-start(f32[2,23,512]{2,0,1:T(2,128)} %param.36) | copy-start | bytes 282628
  2.3 9.5 %copy-start.4 = (f32[3,20,20]{2,1,0:T(8,128)S(1)}, f32[3,20,20]{2,1,0:T(8,128)}, u32[]{:S(2)}) copy-start(f32[3,20,20]{2,1,0:T(8,128)} %refs_4_.2) | copy-start | bytes 14404
  2.3 9.5 %copy-start.5 = (f32[9,512]{1,0:T(8,128)S(1)}, f32[9,512]{1,0:T(8,128)}, u32[]{:S(2)}) copy-start(f32[9,512]{1,0:T(8,128)} %refs_5_.2) | copy-start | bytes 55300
  2.3 9.5 %copy-start.6 = (f32[3,4,512]{2,1,0:T(4,128)S(1)}, f32[3,4,512]{2,1,0:T(4,128)}, u32[]{:S(2)}) copy-start(f32[3,4,512]{2,1,0:T(4,128)} %refs_4_.3) | copy-start | bytes 73732
  2.3 9.5 %copy-start.7 = (f32[23,20]{1,0:T(8,128)S(1)}, f32[23,20]{1,0:T(8,128)}, u32[]{:S(2)}) copy-start(f32[23,20]{1,0:T(8,128)} %refs_7_.1) | copy-start | bytes 5524
  2.3 9.5 %copy-start.8 = (f32[20,23]{1,0:T(8,128)S(1)}, f32[20,23]{1,0:T(8,128)}, u32[]{:S(2)}) copy-start(f32[20,23]{1,0:T(8,128)} %refs_8_.1) | copy-start | bytes 5524
  2.3 9.5 %copy-start.9 = (f32[20,40]{1,0:T(8,128)S(1)}, f32[20,40]{1,0:T(8,128)}, u32[]{:S(2)}) copy-start(f32[20,40]{1,0:T(8,128)} %refs_9_.1) | copy-start | bytes 9604
  2.3 9.5 %copy-start.10 = (s32[4,512]{1,0:T(4,128)S(1)}, s32[4,512]{1,0:T(4,128)}, u32[]{:S(2)}) copy-start(s32[4,512]{1,0:T(4,128)} %refs_2_.3) | copy-start | bytes 24580
  2.3 9.5 %copy-start.12 = (s32[512]{0:T(512)S(1)}, s32[512]{0:T(512)}, u32[]{:S(2)}) copy-start(s32[512]{0:T(512)} %param.35) | copy-start | bytes 6148
  2.3 9.5 %copy-start.13 = (f32[3,32]{1,0:T(4,128)S(1)}, f32[3,32]{1,0:T(4,128)}, u32[]{:S(2)}) copy-start(f32[3,32]{1,0:T(4,128)} %refs_13_.1) | copy-start | bytes 1156
  2.4 9.5 %copy-start.15 = (f32[2,6]{1,0:T(2,128)S(1)}, f32[2,6]{1,0:T(2,128)}, u32[]{:S(2)}) copy-start(f32[2,6]{1,0:T(2,128)} %refs_1_.3) | copy-start | bytes 148
  2.4 9.5 %copy-start.16 = (f32[32]{0:T(128)S(1)}, f32[32]{0:T(128)}, u32[]{:S(2)}) copy-start(f32[32]{0:T(128)} %refs_0_.3) | copy-start | bytes 388
  2.4 9.5 %copy-start.17 = (s32[32]{0:T(128)S(1)}, s32[32]{0:T(128)}, u32[]{:S(2)}) copy-start(s32[32]{0:T(128)} %param.40) | copy-start | bytes 388
  2.4 9.5 %copy-start.20 = (f32[40,192]{1,0:T(8,128)S(1)}, f32[40,192]{1,0:T(8,128)}, u32[]{:S(2)}) copy-start(f32[40,192]{1,0:T(8,128)} %constant.10.clone.refs_14_) | copy-start | bytes 92164
  2.4 9.5 %copy-start.21 = (f32[16,512]{1,0:T(8,128)S(1)}, f32[16,512]{1,0:T(8,128)}, u32[]{:S(2)}) copy-start(f32[16,512]{1,0:T(8,128)} %constant.12.clone.refs_16_.refs_18_) | copy-start | bytes 98308
  2.4 9.5 %copy-start.24 = (f32[23,96]{1,0:T(8,128)S(1)}, f32[23,96]{1,0:T(8,128)}, u32[]{:S(2)}) copy-start(f32[23,96]{1,0:T(8,128)} %constant.11.clone.refs_15_) | copy-start | bytes 26500
  3.3 14.2 %collective-permute-start = (f32[96,128]{1,0:T(8,128)S(1)}, f32[96,128]{1,0:T(8,128)S(1)}, u32[]{:S(2)}, u32[]{:S(2)}) collective-permute-start(f32[96,128]{1,0:T(8,128)S(1)} %get-tuple-element.23), channel_id=1, source_target_pairs={{0,1},{1,2},{2,3},{3,4},{4,5},{5,6},{6,7},{7,8},{8,9},{9,10},{10,1... | collective-permute-start | bytes 147464 | tf_op jit(solution)/shard_map/ppermute | solution.py:612
  7.4 10.2 %collective-permute-start.1 = (f32[96,128]{1,0:T(8,128)S(1)}, f32[96,128]{1,0:T(8,128)S(1)}, u32[]{:S(2)}, u32[]{:S(2)}) collective-permute-start(f32[96,128]{1,0:T(8,128)S(1)} %get-tuple-element.24), channel_id=1, source_target_pairs={{1,0},{2,1},{3,2},{4,3},{5,4},{6,5},{7,6},{8,7},{9,8},{10,9},{11,1... | collective-permute-start | bytes 147464 | tf_op jit(solution)/shard_map/ppermute | solution.py:613
  11.9 5.6 %copy-start.1 = (f32[6,20,512]{2,1,0:T(8,128)S(1)}, f32[6,20,512]{2,1,0:T(8,128)}, u32[]{:S(2)}) copy-start(f32[6,20,512]{2,1,0:T(8,128)} %refs_12_.1) | copy-start | bytes 737284
  11.9 5.6 %copy-start.2 = (f32[32,12,32]{2,0,1:T(8,128)S(1)}, f32[32,12,32]{2,0,1:T(8,128)}, u32[]{:S(2)}) copy-start(f32[32,12,32]{2,0,1:T(8,128)} %param.39) | copy-start | bytes 147460
  11.9 5.6 %copy-start.11 = (f32[4,512]{1,0:T(4,128)S(1)}, f32[4,512]{1,0:T(4,128)}, u32[]{:S(2)}) copy-start(f32[4,512]{1,0:T(4,128)} %refs_5_.3) | copy-start | bytes 24580
  12.0 5.6 %copy-start.18 = (s32[32,1]{0,1:T(1,128)S(1)}, s32[32,1]{0,1:T(1,128)}, u32[]{:S(2)}) copy-start(s32[32,1]{0,1:T(1,128)} %param.41) | copy-start | bytes 388
  12.0 5.6 %copy-start.19 = (f32[32]{0:T(128)S(1)}, f32[32]{0:T(128)}, u32[]{:S(2)}) copy-start(f32[32]{0:T(128)} %param.44) | copy-start | bytes 388
  12.0 5.6 %copy-start.22 = (f32[32,256]{1,0:T(8,128)S(1)}, f32[32,256]{1,0:T(8,128)}, u32[]{:S(2)}) copy-start(f32[32,256]{1,0:T(8,128)} %constant.14.clone.refs_17_) | copy-start | bytes 98308
  12.0 5.6 %copy-start.23 = (f32[32,4]{1,0:T(8,128)S(1)}, f32[32,4]{1,0:T(8,128)}, u32[]{:S(2)}) copy-start(f32[32,4]{1,0:T(8,128)} %constant.13.clone.refs_16_) | copy-start | bytes 1540

commit v3 on v2

--- a/solution.py
+++ b/solution.py
@@ -249,14 +249,116 @@
     upper_ref[...] = total[1][:96] + total[1][96:]
 
 
+def lane_faces():
+    return lax.shift_right_logical(lax.broadcasted_iota(jnp.int32, (1, 128), 1), 5)
+
+
+def fold(values):
+    row = lax.broadcasted_iota(jnp.int32, (128, 128), 0)
+    column = lax.broadcasted_iota(jnp.int32, (128, 128), 1)
+    same = jnp.where((row & (HDEV - 1)) == (column & (HDEV - 1)), 1.0, 0.0).astype(bf16)
+    high, low = high_low(values)
+    return mm(high, same) + mm(low, same)
+
+
+def project_far(dirs_ref, real, imag):
+    theta = [dirs_ref[3 + k : 4 + k, :] for k in range(3)]
+    phi = [dirs_ref[6 + k : 7 + k, :] for k in range(2)]
+
+    def onto_theta(v):
+        return theta[0] * v[0] + theta[1] * v[1] + theta[2] * v[2]
+
+    def onto_phi(v):
+        return phi[0] * v[0] + phi[1] * v[1]
+
+    return (
+        onto_theta(real[:3]) + onto_phi(real[3:]),
+        onto_theta(imag[:3]) + onto_phi(imag[3:]),
+        onto_theta(real[3:]) - onto_phi(real[:3]),
+        onto_theta(imag[3:]) - onto_phi(imag[:3]),
+    )
+
+
+def at(values, i):
+    return values[i * 8 : (i + 1) * 8]
+
+
+def own_frequency(rows):
+    return (lax.broadcasted_iota(jnp.int32, (rows, 256), 0) & 7) == lax.shift_right_logical(
+        lax.broadcasted_iota(jnp.int32, (rows, 256), 1), 5
+    )
+
+
+def fluxes(jump, n, half):
+    e = [jump[i * 16 : (i + 1) * 16] for i in range(3)]
+    h = [jump[i * 16 : (i + 1) * 16] for i in range(3, 6)]
+    normal_e = n[0] * e[0] + n[1] * e[1] + n[2] * e[2]
+    normal_h = n[0] * h[0] + n[1] * h[1] + n[2] * h[2]
+    flux_e, flux_h = [], []
+    for i in range(3):
+        a, b = (i + 1) % 3, (i + 2) % 3
+        flux_e.append((n[a] * h[b] - n[b] * h[a] + e[i] - normal_e * n[i]) * half)
+        flux_h.append((n[b] * e[a] - n[a] * e[b] + h[i] - normal_h * n[i]) * half)
+    return flux_e + flux_h
+
+
+def curls(slope, field_of, metric_of):
+    slope_high, slope_low = high_low(slope)
+    grads = []
+    for c in range(6):
+        high, low = high_low(field_of(c))
+        grads.append(mm(slope_high, high) + (mm(slope_low, high) + mm(slope_high, low)))
+
+    def along(k, c):
+        return (
+            metric_of(k) * grads[c][0:32]
+            + metric_of(3 + k) * grads[c][32:64]
+            + metric_of(6 + k) * grads[c][64:96]
+        )
+
+    return [
+        along(1, 5) - along(2, 4),
+        along(2, 3) - along(0, 5),
+        along(0, 4) - along(1, 3),
+        along(2, 1) - along(1, 2),
+        along(0, 2) - along(2, 0),
+        along(1, 0) - along(0, 1),
+    ]
+
+
+def inverse_of(table_ref, m, material):
+    base = jnp.zeros(material.shape, f32)
+    for k in range(MATS):
+        base = jnp.where(material == k, table_ref[m, k], base)
+    return base
+
+
+def halo_operands(below_ref, above_ref):
+    below_high, below_low = high_low(below_ref[...])
+    above_high, above_low = high_low(above_ref[...])
+    return (
+        jnp.concatenate([below_high, below_low], axis=0),
+        jnp.concatenate([above_high, above_low], axis=0),
+    )
+
+
+def met_at_halo(below, above, mate):
+    met = mm(below, one_hot_rows(SHARED, 4 * ELEMS, mate)) + mm(
+        above, one_hot_rows(SHARED, 4 * ELEMS + SHARED, mate)
+    )
+    return met[:96] + met[96:]
+
+
 def early_kernel(
     wave_ref,
     table_ref,
     fields_ref,
+    res_ref,
     partner_ref,
     derivative_ref,
     geometry_ref,
     normals_ref,
+    scale_ref,
     interp_ref,
     project_ref,
     lift_ref,
@@ -267,16 +369,23 @@
     widen_ref,
     widen_q_ref,
     dirs_ref,
+    spread_ref,
+    spectra_ref,
     trace_ref,
     phase_ref,
+    far_ref,
     jump_ref,
     curl_ref,
     weight_ref,
+    fields_out,
+    res_out,
+    rows_ref,
     lift_out_ref,
     project_out_ref,
-    normal_out_ref,
+    slope_ref,
     pad_ref,
-    grad_ref,
+    stack_ref,
+    group_ref,
 ):
     heading = dirs_ref[...]
     pos = pos_ref[...]
@@ -289,51 +398,97 @@
         for place, half in enumerate(high_low(cos_part) + high_low(sin_part)):
             phase_ref[f // 8, place, rows, :] = half
 
-    slots = slots_ref[...]
-    pick = one_hot_rows(ELEMS, 0, slots & (ELEMS - 1))
+    for i in range(12):
+        came = spectra_ref[i]
+        for g in range(GROUPS):
+            group_ref[g, i * 8 : (i + 1) * 8, :] = came[g * 8 : (g + 1) * 8]
+    spread = spread_ref[...].astype(bf16)
+    own = own_frequency(192)
+    for g in range(GROUPS):
+        high, low = high_low(group_ref[g])
+        rows = jnp.where(own, mm(jnp.concatenate([high, low], axis=0), spread), 0.0).astype(bf16)
+        cos_sum = mm(rows, phase_ref[g, 0])
+        cos_sum = cos_sum[:96] + (cos_sum[96:] + mm(rows[:96], phase_ref[g, 1]))
+        sin_sum = mm(rows, phase_ref[g, 2])
+        sin_sum = sin_sum[:96] + (sin_sum[96:] + mm(rows[:96], phase_ref[g, 3]))
+        real = [at(cos_sum, i) - at(sin_sum, i + 6) for i in range(6)]
+        imag = [at(sin_sum, i) + at(cos_sum, i + 6) for i in range(6)]
+        for c, part in enumerate(project_far(dirs_ref, real, imag)):
+            far_ref[c * FREQS + g * 8 : c * FREQS + (g + 1) * 8, :] = part
+
+    lane_face = lane_faces()
+    tile = jnp.where(
+        (lax.broadcasted_iota(jnp.int32, (HDEV, 128), 1) & (HDEV - 1))
+        == lax.broadcasted_iota(jnp.int32, (HDEV, 128), 0),
+        1.0,
+        0.0,
+    )
+    slots = mm_exact(jnp.broadcast_to(slots_ref[...].astype(f32), (8, HDEV)), tile)[0:1]
+    slots = (slots + 0.5).astype(jnp.int32)
+    element = slots & (ELEMS - 1)
     face_id = lax.shift_right_logical(slots, 9)
-    match = lax.broadcasted_iota(jnp.int32, (4, HDEV), 0) == face_id
-    normal_out_ref[...] = jnp.zeros((8, HDEV), f32)
+    pick = one_hot_rows(ELEMS, 0, element)
+
+    def take(values):
+        high, low = high_low(values)
+        return mm(high, pick) + mm(low, pick)
+
+    stack_ref[...] = jnp.zeros(stack_ref.shape, f32)
     for k in range(3):
-        high, low = high_low(normals_ref[k])
-        normal_out_ref[k : k + 1, :] = jnp.sum(
-            jnp.where(match, mm(high, pick) + mm(low, pick), 0.0), axis=0, keepdims=True
-        )
+        stack_ref[4 * k : 4 * k + 4, :] = normals_ref[k]
+    stack_ref[12:16, :] = scale_ref[...]
+    stack_ref[16:20, :] = partner_ref[...].astype(f32)
+    stack_ref[24:33, :] = geometry_ref[...]
+    stack_ref[33:34, :] = materials_ref[...].astype(f32)
+    taken = take(stack_ref[...])
+
+    def by_face(first):
+        one = lax.broadcasted_iota(jnp.int32, (4, 128), 0) == lane_face
+        return jnp.sum(jnp.where(one, taken[first : first + 4], 0.0), axis=0, keepdims=True)
+
+    normal = [by_face(4 * k) for k in range(3)]
+    mate_row = by_face(16)
+    mate = (mate_row + 0.5).astype(jnp.int32)
+    material = (taken[33:34] + 0.5).astype(jnp.int32)
+    rows_ref[...] = jnp.zeros(rows_ref.shape, f32)
+    for k in range(3):
+        rows_ref[k : k + 1, :] = normal[k]
+        rows_ref[8 + k : 9 + k, :] = jnp.where(lane_face == face_id, normal[k], 0.0)
+    rows_ref[8:16, :] = fold(rows_ref[8:16, :])
+    rows_ref[3:4, :] = 0.5 * by_face(12)
+    rows_ref[4:5, :] = mate_row
+    rows_ref[5:6, :] = face_id.astype(f32)
+    for c in range(6):
+        fields_out[c] = take(fields_ref[c])
+        res_out[c] = take(res_ref[c])
+    for m in range(2):
+        weight_ref[m] = jnp.zeros((32, 128), f32)
+        weight_ref[m, 0:QPTS, :] = take(profile_ref[:, m, :]) * inverse_of(table_ref, m, material)
 
     interp = interp_ref[...]
-    pad_ref[...] = jnp.zeros((96, NP), f32)
+    slope_ref[...] = jnp.zeros((96, NP), f32)
     for r in range(3):
-        pad_ref[r * 32 : r * 32 + QPTS, :] = mm_exact(interp, derivative_ref[r])
-    slope_high, slope_low = high_low(pad_ref[...])
-    for c in range(6):
-        high, low = high_low(fields_ref[c])
-        grad_ref[c] = mm(slope_high, high) + (mm(slope_low, high) + mm(slope_high, low))
-
-    def along(k, c):
-        return (
-            geometry_ref[k : k + 1, :] * grad_ref[c, 0:32, :]
-            + geometry_ref[3 + k : 4 + k, :] * grad_ref[c, 32:64, :]
-            + geometry_ref[6 + k : 7 + k, :] * grad_ref[c, 64:96, :]
-        )
-
-    curl_ref[0] = along(1, 5) - along(2, 4)
-    curl_ref[1] = along(2, 3) - along(0, 5)
-    curl_ref[2] = along(0, 4) - along(1, 3)
-    curl_ref[3] = along(2, 1) - along(1, 2)
-    curl_ref[4] = along(0, 2) - along(2, 0)
-    curl_ref[5] = along(1, 0) - along(0, 1)
-
-    material = materials_ref[...]
-    for m in range(2):
-        base = jnp.zeros((1, ELEMS), f32)
-        for k in range(MATS):
-            base = jnp.where(material == k, table_ref[m, k], base)
-        weight_ref[m] = jnp.zeros((32, ELEMS), f32)
-        weight_ref[m, 0:QPTS, :] = profile_ref[:, m, :] * base
-
-    pad_ref[0:32, :] = jnp.zeros((32, NP), f32)
+        slope_ref[r * 32 : r * 32 + QPTS, :] = mm_exact(interp, derivative_ref[r])
+    for c, curl in enumerate(
+        curls(slope_ref[...], lambda c: fields_out[c], lambda k: taken[24 + k : 25 + k])
+    ):
+        curl_ref[c] = curl
+
+    inside = jnp.zeros((192, 128), f32)
+    outside = jnp.zeros((192, 128), f32)
+    for face in range(4):
+        held = trace_ref[:, face * ELEMS : (face + 1) * ELEMS]
+        inside = inside + jnp.where(lane_face == face, mm(held, pick), 0.0)
+        outside = outside + mm(held, one_hot_rows(ELEMS, face * ELEMS, mate))
+    inside = inside[:96] + inside[96:]
+    outside = outside[:96] + outside[96:]
+    skin = mate == lane_face * ELEMS + element
+    jump_ref[:48, :] = jnp.where(skin, -inside[:48], outside[:48]) - inside[:48]
+    jump_ref[48:, :] = outside[48:] - inside[48:]
+
+    pad_ref[...] = jnp.zeros((32, NP), f32)
     pad_ref[0:QPTS, :] = interp
-    lifted = mm_exact(pad_ref[0:32, :], mm_exact(lift_ref[...], widen_ref[...]))
+    lifted = mm_exact(pad_ref[...], mm_exact(lift_ref[...], widen_ref[...]))
     high, low = high_low(lifted)
     column = lax.broadcasted_iota(jnp.int32, (32, 192), 1)
     lift_out_ref[...] = jnp.where(column < 128, high.astype(f32), low.astype(f32)).astype(bf16)
@@ -342,6 +497,150 @@
     column = lax.broadcasted_iota(jnp.int32, (NP, 96), 1)
     project_out_ref[...] = jnp.where(column < 64, high.astype(f32), low.astype(f32)).astype(bf16)
 
+
+def late_kernel(
+    below_ref,
+    above_ref,
+    rows_ref,
+    jump_ref,
+    curl_ref,
+    weight_ref,
+    lift_ref,
+    project_ref,
+    fields_ref,
+    res_ref,
+    workers_ref,
+    phase_time_ref,
+    on_face_ref,
+    spread_ref,
+    dirs_ref,
+    spectra_ref,
+    phase_ref,
+    came_ref,
+    spectra_out,
+    far_out,
+    current_out,
+    flux_ref,
+    lifted_ref,
+    points_ref,
+    far_ref,
+):
+    lane_face = lane_faces()
+    below, above = halo_operands(below_ref, above_ref)
+    mate = (rows_ref[4:5, :] + 0.5).astype(jnp.int32)
+    jump = jump_ref[...] + met_at_halo(below, above, mate)
+    normal = [rows_ref[k : k + 1, :] for k in range(3)]
+    for c, flux in enumerate(fluxes(jump, normal, rows_ref[3:4, :])):
+        lanes = slice(c * 128, (c + 1) * 128)
+        for face in range(4):
+            high, low = high_low(jnp.where(lane_face == face, flux, 0.0))
+            flux_ref[face * 16 : (face + 1) * 16, lanes] = high
+            flux_ref[64 + face * 16 : 64 + (face + 1) * 16, lanes] = low
+            flux_ref[128 + face * 16 : 128 + (face + 1) * 16, lanes] = high
+    lifted = mm(lift_ref[...], flux_ref[...])
+    for c in range(6):
+        lifted_ref[c * 32 : (c + 1) * 32, :] = lifted[:, c * 128 : (c + 1) * 128]
+    lifted_ref[...] = fold(lifted_ref[...])
+    for c in range(6):
+        lanes = slice(c * 128, (c + 1) * 128)
+        values = (curl_ref[c] + lifted_ref[c * 32 : (c + 1) * 32, :]) * weight_ref[c // 3]
+        high, low = high_low(values)
+        points_ref[0:32, lanes] = high
+        points_ref[32:64, lanes] = low
+        points_ref[64:96, lanes] = high
+    adjusted = mm(project_ref[...], points_ref[...])
+
+    face_id = (rows_ref[5:6, :] + 0.5).astype(jnp.int32)
+    on_face = on_face_ref[...]
+    mask = jnp.zeros((NP, 128), f32)
+    for face in range(4):
+        mask = jnp.where(face_id == face, on_face[:NP, face : face + 1], mask)
+    mean = []
+    for c in range(6):
+        new_res = rk_alpha * res_ref[c] + time_step * adjusted[:, c * 128 : (c + 1) * 128]
+        new_fields = fields_ref[c] + rk_beta * new_res
+        mean.append(jnp.sum(new_fields * mask, axis=0, keepdims=True) * (1.0 / NFP))
+    n = [rows_ref[8 + k : 9 + k, :] for k in range(3)]
+    current_out[...] = jnp.zeros(current_out.shape, f32)
+    current = []
+    for sign, field in ((1.0, mean[3:]), (-1.0, mean[:3])):
+        for i in range(3):
+            a, b = (i + 1) % 3, (i + 2) % 3
+            row = ((n[a] * field[b] - n[b] * field[a]) * sign)[:, :HDEV]
+            current_out[len(current) : len(current) + 1, :] = row
+            current.append(row)
+
+    cos_time, sin_time = cos_sin_turns(phase_time_ref[...] * (0.5 / math.pi))
+    turn = (column_of(cos_time), column_of(sin_time))
+    for i in range(12):
+        spectra_out[i] = spectra_ref[i] + turn[i // 6] * current[i % 6]
+    spectra_out.send()
+
+    workers = workers_ref[...].astype(f32)
+    same = column_of(workers) == workers
+    earlier = lax.broadcasted_iota(jnp.int32, (HDEV, HDEV), 0) < lax.broadcasted_iota(
+        jnp.int32, (HDEV, HDEV), 1
+    )
+    rank = jnp.sum(jnp.where(same & earlier, 1.0, 0.0), axis=0, keepdims=True)
+    target = (rank * GRP + workers).astype(jnp.int32)
+    placing = one_hot_rows(GRP * CAP, 0, target)
+    nt = (((1,), (1,)), ((), ()))
+    high, low = high_low(spectra_out[...].reshape(12 * FREQS, HDEV))
+    placed = lax.dot_general(placing, high, nt, preferred_element_type=f32) + lax.dot_general(
+        placing, low, nt, preferred_element_type=f32
+    )
+    for j in range(3):
+        far_out[pl.ds(CHUNK + j, MEMBERS, stride=ROWS), :] = placed[:, j * 128 : (j + 1) * 128]
+
+    high, low = high_low(current_out[...])
+    tiled = mm(jnp.concatenate([high, low], axis=0), spread_ref[...].astype(bf16))
+    own = own_frequency(8)
+    rows = [jnp.where(own, tiled[i : i + 1], 0.0) for i in range(6)]
+    rows += [jnp.where(own, tiled[8 + i : 9 + i], 0.0) for i in range(6)]
+    rows = jnp.concatenate(rows, axis=0).astype(bf16)
+    for g in range(GROUPS):
+        cos_sum = mm(rows, phase_ref[g, 0])
+        cos_sum = cos_sum[:48] + (cos_sum[48:] + mm(rows[:48], phase_ref[g, 1]))
+        sin_sum = mm(rows, phase_ref[g, 2])
+        sin_sum = sin_sum[:48] + (sin_sum[48:] + mm(rows[:48], phase_ref[g, 3]))
+        cos_turn, sin_turn = at(turn[0], g), at(turn[1], g)
+        real = [cos_turn * at(cos_sum, i) - sin_turn * at(sin_sum, i) for i in range(6)]
+        imag = [cos_turn * at(sin_sum, i) + sin_turn * at(cos_sum, i) for i in range(6)]
+        for c, part in enumerate(project_far(dirs_ref, real, imag)):
+            rows_of = slice(c * FREQS + g * 8, c * FREQS + (g + 1) * 8)
+            far_ref[rows_of, :] = came_ref[rows_of, :] + part
+    far = far_ref[...].T
+    for r in range(CHUNK):
+        far_out[pl.ds(r, MEMBERS, stride=ROWS), :] = far[r * MEMBERS : (r + 1) * MEMBERS]
+
+
+def bulk_kernel(
+    table_ref,
+    current_ref,
+    below_ref,
+    above_ref,
+    fields_ref,
+    res_ref,
+    partner_ref,
+    geometry_ref,
+    normals_ref,
+    scale_ref,
+    materials_ref,
+    profile_ref,
+    trace_ref,
+    lift_ref,
+    project_ref,
+    slope_ref,
+    fields_out,
+    res_out,
+    mark_ref,
+    flux_ref,
+    points_ref,
+    weight_ref,
+):
+    mark_ref[...] = current_ref[...]
+    flux_ref[...] = jnp.zeros(flux_ref.shape, bf16)
+    below, above = halo_operands(below_ref, above_ref)
     for face in range(4):
         lanes = slice(face * ELEMS, (face + 1) * ELEMS)
         mate = partner_ref[face : face + 1, :]
@@ -349,179 +648,41 @@
         for source in range(4):
             held = trace_ref[:, source * ELEMS : (source + 1) * ELEMS]
             total = total + mm(held, one_hot_rows(ELEMS, source * ELEMS, mate))
-        outside = total[:96] + total[96:]
+        outside = total[:96] + total[96:] + met_at_halo(below, above, mate)
         own = trace_ref[:, lanes].astype(f32)
         inside = own[:96] + own[96:]
         skin = mate == lax.broadcasted_iota(jnp.int32, (1, ELEMS), 1) + face * ELEMS
-        jump_ref[:48, lanes] = jnp.where(skin, -inside[:48], outside[:48]) - inside[:48]
-        jump_ref[48:, lanes] = outside[48:] - inside[48:]
-
-
-def late_kernel(
-    below_ref,
-    above_ref,
-    partner_ref,
-    jump_ref,
-    normals_ref,
-    scale_ref,
-    curl_ref,
-    weight_ref,
-    lift_ref,
-    project_ref,
-    normal_pick_ref,
-    fields_ref,
-    res_ref,
-    slots_ref,
-    workers_ref,
-    phase_time_ref,
-    on_face_ref,
-    spread_ref,
-    dirs_ref,
-    spectra_ref,
-    phase_ref,
-    fields_out,
-    res_out,
-    spectra_out,
-    far_out,
-    flux_ref,
-    points_ref,
-    nodal_ref,
-    group_ref,
-    far_ref,
-):
-    flux_ref[...] = jnp.zeros(flux_ref.shape, bf16)
-    nodal_ref[...] = jnp.zeros(nodal_ref.shape, f32)
-
-    below_high, below_low = high_low(below_ref[...])
-    above_high, above_low = high_low(above_ref[...])
-    below = jnp.concatenate([below_high, below_low], axis=0)
-    above = jnp.concatenate([above_high, above_low], axis=0)
-    for face in range(4):
-        lanes = slice(face * ELEMS, (face + 1) * ELEMS)
-        mate = partner_ref[face : face + 1, :]
-        met = mm(below, one_hot_rows(SHARED, 4 * ELEMS, mate)) + mm(
-            above, one_hot_rows(SHARED, 4 * ELEMS + SHARED, mate)
+        jump = jnp.concatenate(
+            [jnp.where(skin, -inside[:48], outside[:48]) - inside[:48], outside[48:] - inside[48:]], axis=0
         )
-        jump = jump_ref[:, lanes] + (met[:96] + met[96:])
-        e = [jump[i * 16 : (i + 1) * 16] for i in range(3)]
-        h = [jump[i * 16 : (i + 1) * 16] for i in range(3, 6)]
-        n = [normals_ref[k, face : face + 1, :] for k in range(3)]
+        normal = [normals_ref[k, face : face + 1, :] for k in range(3)]
         half = 0.5 * scale_ref[face : face + 1, :]
-        normal_e = n[0] * e[0] + n[1] * e[1] + n[2] * e[2]
-        normal_h = n[0] * h[0] + n[1] * h[1] + n[2] * h[2]
-        for i in range(3):
-            a, b = (i + 1) % 3, (i + 2) % 3
-            flux_e = (n[a] * h[b] - n[b] * h[a] + e[i] - normal_e * n[i]) * half
-            flux_h = (n[b] * e[a] - n[a] * e[b] + h[i] - normal_h * n[i]) * half
-            for c, flux in ((i, flux_e), (3 + i, flux_h)):
-                high, low = high_low(flux)
-                flux_ref[c, face * 16 : (face + 1) * 16, :] = high
-                flux_ref[c, 64 + face * 16 : 64 + (face + 1) * 16, :] = low
-                flux_ref[c, 128 + face * 16 : 128 + (face + 1) * 16, :] = high
-
+        for c, flux in enumerate(fluxes(jump, normal, half)):
+            high, low = high_low(flux)
+            flux_ref[c, face * 16 : (face + 1) * 16, :] = high
+            flux_ref[c, 64 + face * 16 : 64 + (face + 1) * 16, :] = low
+            flux_ref[c, 128 + face * 16 : 128 + (face + 1) * 16, :] = high
+    material = materials_ref[...]
+    for m in range(2):
+        weight_ref[m] = jnp.zeros((32, ELEMS), f32)
+        weight_ref[m, 0:QPTS, :] = profile_ref[:, m, :] * inverse_of(table_ref, m, material)
+    curl = curls(slope_ref[...], lambda c: fields_ref[c], lambda k: geometry_ref[k : k + 1, :])
     lift = lift_ref[...]
     project = project_ref[...]
     for c in range(6):
-        values = (curl_ref[c] + mm(lift, flux_ref[c])) * weight_ref[c // 3]
+        values = (curl[c] + mm(lift, flux_ref[c])) * weight_ref[c // 3]
         high, low = high_low(values)
         points_ref[c, 0:32, :] = high
         points_ref[c, 32:64, :] = low
         points_ref[c, 64:96, :] = high
         new_res = rk_alpha * res_ref[c] + time_step * mm(project, points_ref[c])
         res_out[c] = new_res
-        new_fields = fields_ref[c] + rk_beta * new_res
-        fields_out[c] = new_fields
-        nodal_ref[c * 32 : c * 32 + NP, :] = new_fields
+        fields_out[c] = fields_ref[c] + rk_beta * new_res
     fields_out.send()
     res_out.send()
 
-    slots = slots_ref[...]
-    pick = one_hot_rows(ELEMS, 0, slots & (ELEMS - 1))
-    face_id = lax.shift_right_logical(slots, 9)
-    high, low = high_low(nodal_ref[...])
-    picked = mm(high, pick) + mm(low, pick)
-    on_face = on_face_ref[...]
-    mask = jnp.zeros((32, HDEV), f32)
-    for face in range(4):
-        mask = jnp.where(face_id == face, on_face[:, face : face + 1], mask)
-    mean = [
-        jnp.sum(picked[c * 32 : (c + 1) * 32] * mask, axis=0, keepdims=True) * (1.0 / NFP)
-        for c in range(6)
-    ]
-    n = [normal_pick_ref[k : k + 1, :] for k in range(3)]
-    electric, magnetic = mean[:3], mean[3:]
-    current = []
-    for sign, field in ((1.0, magnetic), (-1.0, electric)):
-        for i in range(3):
-            a, b = (i + 1) % 3, (i + 2) % 3
-            current.append((n[a] * field[b] - n[b] * field[a]) * sign)
-
-    cos_time, sin_time = cos_sin_turns(phase_time_ref[...] * (0.5 / math.pi))
-    turn = (column_of(cos_time), column_of(sin_time))
-    for i in range(12):
-        updated = spectra_ref[i] + turn[i // 6] * current[i % 6]
-        spectra_out[i] = updated
-        for g in range(GROUPS):
-            group_ref[g, i * 8 : (i + 1) * 8, :] = updated[g * 8 : (g + 1) * 8]
-
-    spectra_out.send()
-
-    workers = workers_ref[...].astype(f32)
-    same = column_of(workers) == workers
-    earlier = lax.broadcasted_iota(jnp.int32, (HDEV, HDEV), 0) < lax.broadcasted_iota(
-        jnp.int32, (HDEV, HDEV), 1
-    )
-    rank = jnp.sum(jnp.where(same & earlier, 1.0, 0.0), axis=0, keepdims=True)
-    target = (rank * GRP + workers).astype(jnp.int32)
-    placing = one_hot_rows(GRP * CAP, 0, target)
-    nt = (((1,), (1,)), ((), ()))
-    high, low = high_low(spectra_out[...].reshape(12 * FREQS, HDEV))
-    placed = lax.dot_general(placing, high, nt, preferred_element_type=f32) + lax.dot_general(
-        placing, low, nt, preferred_element_type=f32
-    )
-    for j in range(3):
-        far_out[pl.ds(CHUNK + j, MEMBERS, stride=ROWS), :] = placed[:, j * 128 : (j + 1) * 128]
-
-    spread = spread_ref[...].astype(bf16)
-    own = (lax.broadcasted_iota(jnp.int32, (192, 256), 0) & 7) == lax.shift_right_logical(
-        lax.broadcasted_iota(jnp.int32, (192, 256), 1), 5
-    )
-    theta = [dirs_ref[3 + k : 4 + k, :] for k in range(3)]
-    phi = [dirs_ref[6 + k : 7 + k, :] for k in range(2)]
-
-    def onto_theta(v):
-        return theta[0] * v[0] + theta[1] * v[1] + theta[2] * v[2]
-
-    def onto_phi(v):
-        return phi[0] * v[0] + phi[1] * v[1]
-
-    for g in range(GROUPS):
-        high, low = high_low(group_ref[g])
-        rows = jnp.where(own, mm(jnp.concatenate([high, low], axis=0), spread), 0.0).astype(bf16)
-        cos_sum = mm(rows, phase_ref[g, 0])
-        cos_sum = cos_sum[:96] + (cos_sum[96:] + mm(rows[:96], phase_ref[g, 1]))
-        sin_sum = mm(rows, phase_ref[g, 2])
-        sin_sum = sin_sum[:96] + (sin_sum[96:] + mm(rows[:96], phase_ref[g, 3]))
-
-        def at(values, i):
-            return values[i * 8 : (i + 1) * 8]
-
-        real = [at(cos_sum, i) - at(sin_sum, i + 6) for i in range(6)]
-        imag = [at(sin_sum, i) + at(cos_sum, i + 6) for i in range(6)]
-        parts = (
-            onto_theta(real[:3]) + onto_phi(real[3:]),
-            onto_theta(imag[:3]) + onto_phi(imag[3:]),
-            onto_theta(real[3:]) - onto_phi(real[:3]),
-            onto_theta(imag[3:]) - onto_phi(imag[:3]),
-        )
-        for c, part in enumerate(parts):
-            far_ref[c * FREQS + g * 8 : c * FREQS + (g + 1) * 8, :] = part
-    far = far_ref[...].T
-    for r in range(CHUNK):
-        far_out[pl.ds(r, MEMBERS, stride=ROWS), :] = far[r * MEMBERS : (r + 1) * MEMBERS]
-
-
-def sum_kernel(arrived_ref, sum_ref, pieces_ref):
+
+def sum_kernel(arrived_ref, mark_ref, sum_ref, pieces_ref):
     rows = [
         jnp.sum(arrived_ref[pl.ds(r, MEMBERS, stride=ROWS), :], axis=0, keepdims=True) for r in range(CHUNK)
     ]
@@ -612,90 +773,127 @@
     from_below = lax.ppermute(upper, ring, [(i, i + 1) for i in range(partitions - 1)])
     from_above = lax.ppermute(lower, ring, [(i + 1, i) for i in range(partitions - 1)])
 
-    phases, jump, curl, weight, lift3, project3, normal_pick = call(
+    partner = face_partner
+    material_row = materials.reshape(1, ELEMS)
+    coating = profile.transpose(1, 0, 2)
+    came = spectra.transpose(1, 0, 2)
+    phases, far_came, jump, curl, weight, fields_at, res_at, rows, lift3, project3, slope = call(
         early_kernel,
         "early",
         (
             wavenumber,
             mat_table,
             fields,
-            face_partner,
+            section_res,
+            partner,
             derivative,
             geometry,
             normals,
+            face_scale,
             interp_q,
             project_q,
             lift_matrix,
-            materials.reshape(1, ELEMS),
-            profile.transpose(1, 0, 2),
+            material_row,
+            coating,
             slots_row,
             huy_pos,
             widen,
             widen_q,
             directions,
+            spread,
+            came,
             traces,
         ),
         2,
         0,
         (
             sds((GROUPS, 4, 8 * HDEV, DIRS), bf16),
-            sds((96, 4 * ELEMS)),
-            sds((6, 32, ELEMS)),
-            sds((2, 32, ELEMS)),
+            sds((4 * FREQS, DIRS)),
+            sds((96, 128)),
+            sds((6, 32, 128)),
+            sds((2, 32, 128)),
+            sds((6, NP, 128)),
+            sds((6, NP, 128)),
+            sds((16, 128)),
             sds((32, 192), bf16),
             sds((NP, 96), bf16),
-            sds((8, HDEV)),
+            sds((96, NP)),
         ),
         0,
-        [pltpu.VMEM((96, NP), f32), pltpu.VMEM((6, 96, ELEMS), f32)],
+        [pltpu.VMEM((32, NP), f32), pltpu.VMEM((40, ELEMS), f32), pltpu.VMEM((GROUPS, 96, HDEV), f32)],
         PART,
-        10,
-    )
-
-    new_fields, new_res, spectra_t, message = call(
+        6,
+    )
+
+    spectra_t, message, current = call(
         late_kernel,
         "late",
         (
             from_below,
             from_above,
-            face_partner,
+            rows,
             jump,
-            normals,
-            face_scale,
             curl,
             weight,
             lift3,
             project3,
-            normal_pick,
-            fields,
-            section_res,
-            slots_row,
+            fields_at,
+            res_at,
             huy_worker.reshape(1, HDEV),
             time_phase.reshape(1, FREQS),
             on_face,
             spread,
             directions,
-            spectra.transpose(1, 0, 2),
+            came,
             phases,
+            far_came,
         ),
         0,
         0,
+        (sds((12, FREQS, HDEV)), sds((MEMBERS * ROWS, 4 * FREQS)), sds((8, HDEV))),
+        1,
+        [
+            pltpu.VMEM((192, 768), bf16),
+            pltpu.VMEM((192, 128), f32),
+            pltpu.VMEM((96, 768), bf16),
+            pltpu.VMEM((4 * FREQS, DIRS), f32),
+        ],
+        PART,
+        3,
+    )
+
+    new_fields, new_res, mark = call(
+        bulk_kernel,
+        "bulk",
         (
-            sds((6, NP, ELEMS)),
-            sds((6, NP, ELEMS)),
-            sds((12, FREQS, HDEV)),
-            sds((MEMBERS * ROWS, 4 * FREQS)),
+            mat_table,
+            current,
+            from_below,
+            from_above,
+            fields,
+            section_res,
+            partner,
+            geometry,
+            normals,
+            face_scale,
+            material_row,
+            coating,
+            traces,
+            lift3,
+            project3,
+            slope,
         ),
-        3,
+        1,
+        0,
+        (sds((6, NP, ELEMS)), sds((6, NP, ELEMS)), sds((8, HDEV))),
+        2,
         [
             pltpu.VMEM((6, 192, ELEMS), bf16),
             pltpu.VMEM((6, 96, ELEMS), bf16),
-            pltpu.VMEM((192, ELEMS), f32),
-            pltpu.VMEM((GROUPS, 96, HDEV), f32),
-            pltpu.VMEM((4 * FREQS, DIRS), f32),
+            pltpu.VMEM((2, 32, ELEMS), f32),
         ],
         PART,
-        8,
+        6,
     )
     new_spectra = spectra_t.transpose(1, 0, 2)
 
@@ -707,11 +905,11 @@
     part, pieces = pl.pallas_call(
         sum_kernel,
         out_shape=(sds((along_z, CHUNK, 128)), sds((chunks, 3, GRP, 128))),
-        in_specs=[VMEM],
+        in_specs=[VMEM, VMEM],
         out_specs=(VMEM, VMEM),
         name="sum",
         **small,
-    )(arrived)
+    )(arrived, mark)
     part = lax.all_to_all(part, "z", 0, 0, tiled=True)
     message = pl.pallas_call(
         join_kernel,

time: 83.5 us -> 82 us (0.982)
  blocking collectives: 60.3 us -> 36.2 us
  starting transfers between devices: 8.41 us -> 18.7 us
  waiting for transfers between devices: 0.01 us -> 8.73 us
  Pallas kernels: 11.7 us -> 15.2 us
    all_to_all x1 -> x0, blocking collectives: 24 us -> none  [per_device(): lax.all_to_all(message.reshape(MEMBERS, 1, ROWS * 128), ('x', 'core', 'y'...]
    all_to_all x0 -> x1, starting transfers between devices: none -> 10.3 us  [per_device(): lax.all_to_all(message.reshape(MEMBERS, 1, ROWS * 128), ('x', 'core', 'y'...]
    all_to_all x0 -> x1, waiting for transfers between devices: none -> 8.73 us  [per_device(): lax.all_to_all(message.reshape(MEMBERS, 1, ROWS * 128), ('x', 'core', 'y'...]
    pallas_call x3 -> x4, Pallas kernels: 10.8 us -> 14.3 us  [call(): pl.pallas_call(moving(kernel, first, fetched, len(operands), sent, len(ou...]
    unnamed x50 -> x52, local copies, waits for them, and re-layouts: 1.75 us -> 1.75 us
  transfers between devices with their start and end apart: 2 -> 3, of which waited for: 0 -> 1; matrix products, arithmetic and copies ran while one was open for 0% -> 0% of each run, Pallas kernels for 7% -> 13%
where the time goes in v3:
time: 82 us; the launch traced here: 81.7 us
  blocking collectives  36.2 us (44%)
  starting transfers between devices  18.7 us (23%)
  Pallas kernels  15.2 us (19%)
  waiting for transfers between devices  8.73 us (11%)
  local copies, waits for them, and re-layouts  1.75 us (2%)
  between operations  1.07 us (1%)
    all_to_all x1, blocking collectives, per_device(): part = lax.all_to_all(part, 'z', 0, 0, tiled=True)  24.4 us
    pallas_call x4, Pallas kernels, call(): pl.pallas_call(moving(kernel, first, fetched, len(operands), sent, len(ou...  14.3 us
    all_to_all x1, blocking collectives, per_device(): arrived = lax.all_to_all(message, ('x', 'core'), 0, 0, tiled=True)  11.9 us
    all_to_all x1, starting transfers between devices, per_device(): lax.all_to_all(message.reshape(MEMBERS, 1, ROWS * 128), ('x', 'core', 'y'...  10.3 us
    all_to_all x1, waiting for transfers between devices, per_device(): lax.all_to_all(message.reshape(MEMBERS, 1, ROWS * 128), ('x', 'core', 'y'...  8.73 us
    ppermute x1, starting transfers between devices, per_device(): lax.ppermute(lower, ring, [(i + 1, i) for i in range(partitions - 1)])  4.37 us
    ppermute x1, starting transfers between devices, per_device(): lax.ppermute(upper, ring, [(i, i + 1) for i in range(partitions - 1)])  4.04 us
    unnamed x52, local copies, waits for them, and re-layouts  1.75 us
  transfers between devices with their start and end apart: 3, of which 1 were waited for; matrix products, arithmetic and copies ran while one was open for 0% of the time, Pallas kernels for 13%

profile of v3, /device:TPU:1, one launch (start us, length us, event | category | flops | bytes accessed | tf_op | source)
XLA Modules:
  0.0 81.7 jit_solution(9115700230799114604)
XLA Ops:
  0.6 0.0 copy-start
  0.7 1.0 %copy-done = f32[6,20,512]{2,1,0:T(8,128)S(1)} copy-done((f32[6,20,512]{2,1,0:T(8,128)S(1)}, f32[6,20,512]{2,1,0:T(8,128)}, u32[]{:S(2)}) %copy-start) | copy-done | bytes 245784
  1.6 0.7 copy-done.15
  2.4 0.0 copy-start.21
  2.4 0.0 copy-start.22
  2.4 0.0 copy-start.23
  2.5 0.0 copy-start.25
  2.5 0.9 %traces.1 = (bf16[192,2048]{1,0:T(8,128)(2,1)S(1)}, f32[96,128]{1,0:T(8,128)S(1)}, f32[96,128]{1,0:T(8,128)S(1)}) custom-call(f32[6,20,512]{2,1,0:T(8,128)S(1)} %copy-done, s32[2,128]{1,0:T(2,128)S(1)} %copy-done.15), custom_call_target="tpu_custom_call" | custom-call | flops 2300000000 | bytes 4194304 | tf_op jit(solution)/shard_map/traces/pallas_call | solution.py:214
  3.4 4.0 %collective-permute-start = (f32[96,128]{1,0:T(8,128)S(1)}, f32[96,128]{1,0:T(8,128)S(1)}, u32[]{:S(2)}, u32[]{:S(2)}) collective-permute-start(f32[96,128]{1,0:T(8,128)S(1)} %get-tuple-element.29), channel_id=1, source_target_pairs={{0,1},{1,2},{2,3},{3,4},{4,5},{5,6},{6,7},{7,8},{8,9},{9,10},{10,1... | collective-permute-start | bytes 147464 | tf_op jit(solution)/shard_map/ppermute | solution.py:773
  7.4 4.4 %collective-permute-start.1 = (f32[96,128]{1,0:T(8,128)S(1)}, f32[96,128]{1,0:T(8,128)S(1)}, u32[]{:S(2)}, u32[]{:S(2)}) collective-permute-start(f32[96,128]{1,0:T(8,128)S(1)} %get-tuple-element.30), channel_id=1, source_target_pairs={{1,0},{2,1},{3,2},{4,3},{5,4},{6,5},{7,6},{8,7},{9,8},{10,9},{11,1... | collective-permute-start | bytes 147464 | tf_op jit(solution)/shard_map/ppermute | solution.py:774
  11.8 0.0 copy-done.2
  11.8 0.0 copy-done.3
  11.8 0.0 copy-done.4
  11.8 0.0 copy-done.5
  11.8 0.0 copy-done.6
  11.9 0.0 copy-done.7
  11.9 0.0 copy-done.8
  11.9 0.0 copy-done.9
  12.0 0.0 copy-start.19
  12.0 0.0 copy-start.20
  12.0 0.0 copy-start.24
  12.0 5.5 %early.1 = (bf16[4,4,256,512]{3,2,1,0:T(8,128)(2,1)S(1)}, f32[128,512]{1,0:T(8,128)S(1)}, f32[96,128]{1,0:T(8,128)S(1)}, f32[6,32,128]{2,1,0:T(8,128)S(1)}, f32[...) custom-call(f32[32]{0:T(128)S(1)} %copy-done.17, ...), custom_call_target="tpu_custom_call" | custom-call | flops 6899999744 | bytes 4194304 | tf_op jit(solution)/shard_map/early/pallas_call | solution.py:214
  17.5 0.0 collective-permute-done.refs_0_.refs_2_
  17.5 0.0 collective-permute-done.1.refs_1_.refs_3_
  17.6 0.0 copy-start.1
  17.6 2.7 %late.1 = (f32[12,32,32]{2,1,0:T(8,128)}, f32[704,128]{1,0:T(8,128)}, f32[8,32]{1,0:T(8,128)S(1)}) custom-call(f32[96,128]{1,0:T(8,128)S(1)} %collective-permute-done.refs_0_.refs_2_, f32[96,128]{1,0:T(8,128)S(1)} %collective-permute-done.1.refs_1_.refs_3_, f32[16,128]{1,0:T(8,128)S(1)} %get-tuple-element.32.refs_2_, ...), custom_call_target="tpu_custom_call" | custom-call | flops 3449999872 | bytes 4194304 | tf_op jit(solution)/shard_map/late/pallas_call | solution.py:214
  20.3 10.3 %all-to-all-start = ((f32[64,1,1408]{2,1,0:T(1,128)}), f32[64,1,1408]{2,1,0:T(1,128)S(1)}, u32[]{:S(2)}, u32[]{:S(2)}) async-start(f32[64,1,1408]{2,1,0:T(1,128)} %bitcast.7), calls=%async_computation | async-start | bytes 720896 | tf_op jit(solution)/shard_map/all_to_all | solution.py:902
  30.6 5.2 %bulk.1 = (f32[6,20,512]{2,1,0:T(8,128)}, f32[6,20,512]{2,1,0:T(8,128)}, f32[8,32]{1,0:T(8,128)S(1)}) custom-call(f32[2,6]{1,0:T(2,128)S(1)} %copy-done.16, f32[8,32]{1,0:T(8,128)S(1)} %get-tuple-element.42.refs_1_, f32[96,128]{1,0:T(8,128)S(1)} %collective-permute-done.refs_0_.refs_2_, f32[96,128]{1,0:T(8,128)S(1)} %collective-permute-done.1.refs_1_.refs_3_, ...), custom_call_target="tpu_custom_call" | custom-call | flops 6899999744 | bytes 4194304 | tf_op jit(solution)/shard_map/bulk/pallas_call | solution.py:214
  35.8 8.7 %all-to-all-done = f32[64,1,1408]{2,1,0:T(1,128)S(1)} async-done(((f32[64,1,1408]{2,1,0:T(1,128)}), f32[64,1,1408]{2,1,0:T(1,128)S(1)}, u32[]{:S(2)}, u32[]{:S(2)}) %all-to-all-start) | async-done | bytes 360480 | tf_op jit(solution)/shard_map/all_to_all | solution.py:902
  44.6 24.4 %all_to_all.15.arrived_ref = f32[12,8,128]{2,1,0:T(8,128)S(1)} all-to-all(f32[12,8,128]{2,1,0:T(8,128)S(1)} %get-tuple-element.49), channel_id=1, replica_groups=mesh['z'=12,'x'=4,'core'=2,'y'=8] {'z'}, dimensions={0} | all-to-all | bytes 98304 | tf_op jit(solution)/shard_map/all_to_all | solution.py:913
  69.0 11.9 %all_to_all.16.arrived_ref = f32[8,4,8,128]{3,2,1,0:T(8,128)S(1)} all-to-all(f32[8,4,8,128]{3,2,1,0:T(8,128)S(1)} %join.1), channel_id=1, replica_groups=mesh['z'=12,'x'=4,'core'=2,'y'=8] {'x','core'}, dimensions={0} | all-to-all | bytes 262144 | tf_op jit(solution)/shard_map/all_to_all | solution.py:922
  80.8 0.8 %final.1 = (f32[64,128]{1,0:T(8,128)}, f32[12,32,64]{2,1,0:T(8,128)}) custom-call(f32[8,4,8,128]{3,2,1,0:T(8,128)S(1)} %all_to_all.16.arrived_ref), custom_call_target="tpu_custom_call" | custom-call | tf_op jit(solution)/shard_map/final/pallas_call | solution.py:923
  (35 shorter events, 0.1 us)
Async XLA Ops:
  0.6 1.0 %copy-start = (f32[6,20,512]{2,1,0:T(8,128)S(1)}, f32[6,20,512]{2,1,0:T(8,128)}, u32[]{:S(2)}) copy-start(f32[6,20,512]{2,1,0:T(8,128)} %refs_4_.3) | copy-start | bytes 737284
  1.6 0.7 copy-start.15
  2.3 9.5 %copy-start.2 = (f32[6,20,512]{2,1,0:T(8,128)S(1)}, f32[6,20,512]{2,1,0:T(8,128)}, u32[]{:S(2)}) copy-start(f32[6,20,512]{2,1,0:T(8,128)} %refs_5_.3) | copy-start | bytes 737284
  2.3 9.5 %copy-start.3 = (f32[32,12,32]{2,0,1:T(8,128)S(1)}, f32[32,12,32]{2,0,1:T(8,128)}, u32[]{:S(2)}) copy-start(f32[32,12,32]{2,0,1:T(8,128)} %param.39) | copy-start | bytes 147460
  2.3 9.5 %copy-start.4 = (f32[2,23,512]{2,0,1:T(2,128)S(1)}, f32[2,23,512]{2,0,1:T(2,128)}, u32[]{:S(2)}) copy-start(f32[2,23,512]{2,0,1:T(2,128)} %param.36) | copy-start | bytes 282628
  2.3 9.5 %copy-start.5 = (f32[3,20,20]{2,1,0:T(8,128)S(1)}, f32[3,20,20]{2,1,0:T(8,128)}, u32[]{:S(2)}) copy-start(f32[3,20,20]{2,1,0:T(8,128)} %refs_5_.2) | copy-start | bytes 14404
  2.3 9.6 %copy-start.6 = (f32[9,512]{1,0:T(8,128)S(1)}, f32[9,512]{1,0:T(8,128)}, u32[]{:S(2)}) copy-start(f32[9,512]{1,0:T(8,128)} %refs_7_.3) | copy-start | bytes 55300
  2.3 9.6 %copy-start.7 = (f32[3,4,512]{2,1,0:T(4,128)S(1)}, f32[3,4,512]{2,1,0:T(4,128)}, u32[]{:S(2)}) copy-start(f32[3,4,512]{2,1,0:T(4,128)} %refs_8_.3) | copy-start | bytes 73732
  2.3 9.6 %copy-start.8 = (f32[23,20]{1,0:T(8,128)S(1)}, f32[23,20]{1,0:T(8,128)}, u32[]{:S(2)}) copy-start(f32[23,20]{1,0:T(8,128)} %refs_9_.2) | copy-start | bytes 5524
  2.3 9.6 %copy-start.9 = (f32[20,23]{1,0:T(8,128)S(1)}, f32[20,23]{1,0:T(8,128)}, u32[]{:S(2)}) copy-start(f32[20,23]{1,0:T(8,128)} %refs_10_.1) | copy-start | bytes 5524
  2.3 9.6 %copy-start.10 = (f32[20,40]{1,0:T(8,128)S(1)}, f32[20,40]{1,0:T(8,128)}, u32[]{:S(2)}) copy-start(f32[20,40]{1,0:T(8,128)} %refs_11_.1) | copy-start | bytes 9604
  2.3 9.6 %copy-start.11 = (s32[4,512]{1,0:T(4,128)S(1)}, s32[4,512]{1,0:T(4,128)}, u32[]{:S(2)}) copy-start(s32[4,512]{1,0:T(4,128)} %refs_6_.3) | copy-start | bytes 24580
  2.4 9.6 %copy-start.12 = (f32[4,512]{1,0:T(4,128)S(1)}, f32[4,512]{1,0:T(4,128)}, u32[]{:S(2)}) copy-start(f32[4,512]{1,0:T(4,128)} %refs_9_.3) | copy-start | bytes 24580
  2.4 9.6 %copy-start.13 = (f32[3,32]{1,0:T(4,128)S(1)}, f32[3,32]{1,0:T(4,128)}, u32[]{:S(2)}) copy-start(f32[3,32]{1,0:T(4,128)} %refs_15_.1) | copy-start | bytes 1156
  2.4 9.6 %copy-start.14 = (s32[512]{0:T(512)S(1)}, s32[512]{0:T(512)}, u32[]{:S(2)}) copy-start(s32[512]{0:T(512)} %param.35) | copy-start | bytes 6148
  2.4 9.6 %copy-start.16 = (f32[2,6]{1,0:T(2,128)S(1)}, f32[2,6]{1,0:T(2,128)}, u32[]{:S(2)}) copy-start(f32[2,6]{1,0:T(2,128)} %refs_0_.5) | copy-start | bytes 148
  2.4 9.6 %copy-start.17 = (f32[32]{0:T(128)S(1)}, f32[32]{0:T(128)}, u32[]{:S(2)}) copy-start(f32[32]{0:T(128)} %refs_0_.4) | copy-start | bytes 388
  2.4 9.6 %copy-start.18 = (s32[32]{0:T(128)S(1)}, s32[32]{0:T(128)}, u32[]{:S(2)}) copy-start(s32[32]{0:T(128)} %param.40) | copy-start | bytes 388
  2.4 9.6 %copy-start.21 = (f32[40,192]{1,0:T(8,128)S(1)}, f32[40,192]{1,0:T(8,128)}, u32[]{:S(2)}) copy-start(f32[40,192]{1,0:T(8,128)} %constant.10.clone.refs_16_) | copy-start | bytes 92164
  2.4 9.5 %copy-start.22 = (f32[32,256]{1,0:T(8,128)S(1)}, f32[32,256]{1,0:T(8,128)}, u32[]{:S(2)}) copy-start(f32[32,256]{1,0:T(8,128)} %constant.13.clone.refs_19_.refs_13_) | copy-start | bytes 98308
  2.4 9.5 %copy-start.23 = (f32[16,512]{1,0:T(8,128)S(1)}, f32[16,512]{1,0:T(8,128)}, u32[]{:S(2)}) copy-start(f32[16,512]{1,0:T(8,128)} %constant.12.clone.refs_18_.refs_14_) | copy-start | bytes 98308
  2.5 9.5 %copy-start.25 = (f32[23,96]{1,0:T(8,128)S(1)}, f32[23,96]{1,0:T(8,128)}, u32[]{:S(2)}) copy-start(f32[23,96]{1,0:T(8,128)} %constant.11.clone.refs_17_) | copy-start | bytes 26500
  3.4 14.1 %collective-permute-start = (f32[96,128]{1,0:T(8,128)S(1)}, f32[96,128]{1,0:T(8,128)S(1)}, u32[]{:S(2)}, u32[]{:S(2)}) collective-permute-start(f32[96,128]{1,0:T(8,128)S(1)} %get-tuple-element.29), channel_id=1, source_target_pairs={{0,1},{1,2},{2,3},{3,4},{4,5},{5,6},{6,7},{7,8},{8,9},{9,10},{10,1... | collective-permute-start | bytes 147464 | tf_op jit(solution)/shard_map/ppermute | solution.py:773
  7.4 10.1 %collective-permute-start.1 = (f32[96,128]{1,0:T(8,128)S(1)}, f32[96,128]{1,0:T(8,128)S(1)}, u32[]{:S(2)}, u32[]{:S(2)}) collective-permute-start(f32[96,128]{1,0:T(8,128)S(1)} %get-tuple-element.30), channel_id=1, source_target_pairs={{1,0},{2,1},{3,2},{4,3},{5,4},{6,5},{7,6},{8,7},{9,8},{10,9},{11,1... | collective-permute-start | bytes 147464 | tf_op jit(solution)/shard_map/ppermute | solution.py:774
  12.0 5.5 %copy-start.19 = (s32[32,1]{0,1:T(1,128)S(1)}, s32[32,1]{0,1:T(1,128)}, u32[]{:S(2)}) copy-start(s32[32,1]{0,1:T(1,128)} %param.41) | copy-start | bytes 388
  12.0 5.5 %copy-start.20 = (f32[32]{0:T(128)S(1)}, f32[32]{0:T(128)}, u32[]{:S(2)}) copy-start(f32[32]{0:T(128)} %param.44) | copy-start | bytes 388
  12.0 5.5 %copy-start.24 = (f32[32,4]{1,0:T(8,128)S(1)}, f32[32,4]{1,0:T(8,128)}, u32[]{:S(2)}) copy-start(f32[32,4]{1,0:T(8,128)} %constant.14.clone.refs_12_) | copy-start | bytes 1540
  17.6 13.0 %copy-start.1 = (f32[6,20,512]{2,1,0:T(8,128)S(1)}, f32[6,20,512]{2,1,0:T(8,128)}, u32[]{:S(2)}) copy-start(f32[6,20,512]{2,1,0:T(8,128)} %refs_4_.3) | copy-start | bytes 737284
  20.3 24.3 %all-to-all-start = ((f32[64,1,1408]{2,1,0:T(1,128)}), f32[64,1,1408]{2,1,0:T(1,128)S(1)}, u32[]{:S(2)}, u32[]{:S(2)}) async-start(f32[64,1,1408]{2,1,0:T(1,128)} %bitcast.7), calls=%async_computation | async-start | bytes 720896 | tf_op jit(solution)/shard_map/all_to_all | solution.py:902

commit v4 on v3

--- a/solution.py
+++ b/solution.py
@@ -210,7 +210,7 @@
         scratch_shapes.append(pltpu.SemaphoreType.DMA((fetched,)))
     if sent:
         scratch_shapes += [pltpu.VMEM(o.shape, o.dtype) for o in outs[:sent]]
-        scratch_shapes.append(pltpu.SemaphoreType.DMA((sent, GROUPS)))
+        scratch_shapes.append(pltpu.SemaphoreType.DMA((sent, 6)))
     return pl.pallas_call(
         moving(kernel, first, fetched, len(operands), sent, len(outs)),
         out_shape=tuple(outs),
@@ -677,9 +677,9 @@
         points_ref[c, 64:96, :] = high
         new_res = rk_alpha * res_ref[c] + time_step * mm(project, points_ref[c])
         res_out[c] = new_res
+        res_out.send(c)
         fields_out[c] = fields_ref[c] + rk_beta * new_res
-    fields_out.send()
-    res_out.send()
+        fields_out.send(c)
 
 
 def sum_kernel(arrived_ref, mark_ref, sum_ref, pieces_ref):
@@ -694,18 +694,22 @@
         pieces_ref[:, j] = piece.reshape(MEMBERS // GRP, GRP, 128)
 
 
+def core_first(chunk):
+    return chunk % 2 * (MEMBERS // GRP // 2) + chunk // 2
+
+
 def join_kernel(arrived_ref, pieces_ref, message_ref):
     total = jnp.sum(arrived_ref[...], axis=0)
     for p in range(message_ref.shape[0]):
-        message_ref[p, 0] = total
-        message_ref[p, 1:] = pieces_ref[p]
+        message_ref[core_first(p), 0] = total
+        message_ref[core_first(p), 1:] = pieces_ref[p]
 
 
 def final_kernel(arrived_ref, far_ref, worker_ref, rows_ref):
     for p in range(arrived_ref.shape[0]):
-        far_ref[p * CHUNK : (p + 1) * CHUNK, :] = arrived_ref[p, 0]
+        far_ref[p * CHUNK : (p + 1) * CHUNK, :] = arrived_ref[core_first(p), 0]
         for j in range(3):
-            rows_ref[j, pl.ds(p, GRP, stride=CAP), :] = arrived_ref[p, 1 + j]
+            rows_ref[j, pl.ds(p, GRP, stride=CAP), :] = arrived_ref[core_first(p), 1 + j]
     for j in range(3):
         worker_ref[4 * j : 4 * j + 4] = rows_ref[j].T.reshape(4, FREQS, GRP * CAP)
 
@@ -919,7 +923,7 @@
         name="join",
         **small,
     )(part, pieces)
-    arrived = lax.all_to_all(message, ("x", "core"), 0, 0, tiled=True)
+    arrived = lax.all_to_all(message, ("core", "x"), 0, 0, tiled=True)
     far_field, worker_t = pl.pallas_call(
         final_kernel,
         out_shape=(sds((chunks * CHUNK, 128)), sds((12, FREQS, GRP * CAP))),

time: 82 us -> 81.9 us (level)
  no operation moved by 1% of the time
where the time goes in v4:
time: 81.9 us; the launch traced here: 81.6 us
  blocking collectives  36.1 us (44%)
  starting transfers between devices  18.7 us (23%)
  Pallas kernels  15.1 us (18%)
  waiting for transfers between devices  8.86 us (11%)
  local copies, waits for them, and re-layouts  1.75 us (2%)
  between operations  1.07 us (1%)
    all_to_all x1, blocking collectives, per_device(): part = lax.all_to_all(part, 'z', 0, 0, tiled=True)  24.4 us
    pallas_call x4, Pallas kernels, call(): pl.pallas_call(moving(kernel, first, fetched, len(operands), sent, len(ou...  14.2 us
    all_to_all x1, blocking collectives, per_device(): arrived = lax.all_to_all(message, ('core', 'x'), 0, 0, tiled=True)  11.8 us
    all_to_all x1, starting transfers between devices, per_device(): lax.all_to_all(message.reshape(MEMBERS, 1, ROWS * 128), ('x', 'core', 'y'...  10.3 us
    all_to_all x1, waiting for transfers between devices, per_device(): lax.all_to_all(message.reshape(MEMBERS, 1, ROWS * 128), ('x', 'core', 'y'...  8.86 us
    ppermute x1, starting transfers between devices, per_device(): lax.ppermute(lower, ring, [(i + 1, i) for i in range(partitions - 1)])  4.37 us
    ppermute x1, starting transfers between devices, per_device(): lax.ppermute(upper, ring, [(i, i + 1) for i in range(partitions - 1)])  4.04 us
    unnamed x52, local copies, waits for them, and re-layouts  1.75 us
  transfers between devices with their start and end apart: 3, of which 1 were waited for; matrix products, arithmetic and copies ran while one was open for 0% of the time, Pallas kernels for 13%

profile of v4, /device:TPU:1, one launch (start us, length us, event | category | flops | bytes accessed | tf_op | source)
XLA Modules:
  0.0 81.6 jit_solution(10755705517477212639)
XLA Ops:
  0.6 0.0 copy-start
  0.7 1.0 %copy-done = f32[6,20,512]{2,1,0:T(8,128)S(1)} copy-done((f32[6,20,512]{2,1,0:T(8,128)S(1)}, f32[6,20,512]{2,1,0:T(8,128)}, u32[]{:S(2)}) %copy-start) | copy-done | bytes 245784
  1.6 0.7 copy-done.15
  2.4 0.0 copy-start.21
  2.4 0.0 copy-start.22
  2.4 0.0 copy-start.23
  2.5 0.0 copy-start.25
  2.5 0.9 %traces.1 = (bf16[192,2048]{1,0:T(8,128)(2,1)S(1)}, f32[96,128]{1,0:T(8,128)S(1)}, f32[96,128]{1,0:T(8,128)S(1)}) custom-call(f32[6,20,512]{2,1,0:T(8,128)S(1)} %copy-done, s32[2,128]{1,0:T(2,128)S(1)} %copy-done.15), custom_call_target="tpu_custom_call" | custom-call | flops 2300000000 | bytes 4194304 | tf_op jit(solution)/shard_map/traces/pallas_call | solution.py:214
  3.4 4.0 %collective-permute-start = (f32[96,128]{1,0:T(8,128)S(1)}, f32[96,128]{1,0:T(8,128)S(1)}, u32[]{:S(2)}, u32[]{:S(2)}) collective-permute-start(f32[96,128]{1,0:T(8,128)S(1)} %get-tuple-element.29), channel_id=1, source_target_pairs={{0,1},{1,2},{2,3},{3,4},{4,5},{5,6},{6,7},{7,8},{8,9},{9,10},{10,1... | collective-permute-start | bytes 147464 | tf_op jit(solution)/shard_map/ppermute | solution.py:777
  7.4 4.4 %collective-permute-start.1 = (f32[96,128]{1,0:T(8,128)S(1)}, f32[96,128]{1,0:T(8,128)S(1)}, u32[]{:S(2)}, u32[]{:S(2)}) collective-permute-start(f32[96,128]{1,0:T(8,128)S(1)} %get-tuple-element.30), channel_id=1, source_target_pairs={{1,0},{2,1},{3,2},{4,3},{5,4},{6,5},{7,6},{8,7},{9,8},{10,9},{11,1... | collective-permute-start | bytes 147464 | tf_op jit(solution)/shard_map/ppermute | solution.py:778
  11.8 0.0 copy-done.2
  11.8 0.0 copy-done.3
  11.8 0.0 copy-done.4
  11.8 0.0 copy-done.5
  11.8 0.0 copy-done.6
  11.9 0.0 copy-done.7
  11.9 0.0 copy-done.8
  11.9 0.0 copy-done.9
  12.0 0.0 copy-start.19
  12.0 0.0 copy-start.20
  12.0 0.0 copy-start.24
  12.0 5.5 %early.1 = (bf16[4,4,256,512]{3,2,1,0:T(8,128)(2,1)S(1)}, f32[128,512]{1,0:T(8,128)S(1)}, f32[96,128]{1,0:T(8,128)S(1)}, f32[6,32,128]{2,1,0:T(8,128)S(1)}, f32[...) custom-call(f32[32]{0:T(128)S(1)} %copy-done.17, ...), custom_call_target="tpu_custom_call" | custom-call | flops 6899999744 | bytes 4194304 | tf_op jit(solution)/shard_map/early/pallas_call | solution.py:214
  17.5 0.0 collective-permute-done.refs_0_.refs_2_
  17.5 0.0 collective-permute-done.1.refs_1_.refs_3_
  17.6 0.0 copy-start.1
  17.6 2.7 %late.1 = (f32[12,32,32]{2,1,0:T(8,128)}, f32[704,128]{1,0:T(8,128)}, f32[8,32]{1,0:T(8,128)S(1)}) custom-call(f32[96,128]{1,0:T(8,128)S(1)} %collective-permute-done.refs_0_.refs_2_, f32[96,128]{1,0:T(8,128)S(1)} %collective-permute-done.1.refs_1_.refs_3_, f32[16,128]{1,0:T(8,128)S(1)} %get-tuple-element.32.refs_2_, ...), custom_call_target="tpu_custom_call" | custom-call | flops 3449999872 | bytes 4194304 | tf_op jit(solution)/shard_map/late/pallas_call | solution.py:214
  20.3 10.3 %all-to-all-start = ((f32[64,1,1408]{2,1,0:T(1,128)}), f32[64,1,1408]{2,1,0:T(1,128)S(1)}, u32[]{:S(2)}, u32[]{:S(2)}) async-start(f32[64,1,1408]{2,1,0:T(1,128)} %bitcast.7), calls=%async_computation | async-start | bytes 720896 | tf_op jit(solution)/shard_map/all_to_all | solution.py:906
  30.6 5.1 %bulk.1 = (f32[6,20,512]{2,1,0:T(8,128)}, f32[6,20,512]{2,1,0:T(8,128)}, f32[8,32]{1,0:T(8,128)S(1)}) custom-call(f32[2,6]{1,0:T(2,128)S(1)} %copy-done.16, f32[8,32]{1,0:T(8,128)S(1)} %get-tuple-element.42.refs_1_, f32[96,128]{1,0:T(8,128)S(1)} %collective-permute-done.refs_0_.refs_2_, f32[96,128]{1,0:T(8,128)S(1)} %collective-permute-done.1.refs_1_.refs_3_, ...), custom_call_target="tpu_custom_call" | custom-call | flops 6899999744 | bytes 4194304 | tf_op jit(solution)/shard_map/bulk/pallas_call | solution.py:214
  35.7 8.9 %all-to-all-done = f32[64,1,1408]{2,1,0:T(1,128)S(1)} async-done(((f32[64,1,1408]{2,1,0:T(1,128)}), f32[64,1,1408]{2,1,0:T(1,128)S(1)}, u32[]{:S(2)}, u32[]{:S(2)}) %all-to-all-start) | async-done | bytes 360480 | tf_op jit(solution)/shard_map/all_to_all | solution.py:906
  44.6 24.4 %all_to_all.15.arrived_ref = f32[12,8,128]{2,1,0:T(8,128)S(1)} all-to-all(f32[12,8,128]{2,1,0:T(8,128)S(1)} %get-tuple-element.49), channel_id=1, replica_groups=mesh['z'=12,'x'=4,'core'=2,'y'=8] {'z'}, dimensions={0} | all-to-all | bytes 98304 | tf_op jit(solution)/shard_map/all_to_all | solution.py:917
  69.0 11.8 %all_to_all.16.arrived_ref = f32[8,4,8,128]{3,2,1,0:T(8,128)S(1)} all-to-all(f32[8,4,8,128]{3,2,1,0:T(8,128)S(1)} %join.1), channel_id=1, replica_groups=mesh['z'=12,'x'=4,'core'=2,'y'=8] {'core','x'}, dimensions={0} | all-to-all | bytes 262144 | tf_op jit(solution)/shard_map/all_to_all | solution.py:926
  80.7 0.8 %final.1 = (f32[64,128]{1,0:T(8,128)}, f32[12,32,64]{2,1,0:T(8,128)}) custom-call(f32[8,4,8,128]{3,2,1,0:T(8,128)S(1)} %all_to_all.16.arrived_ref), custom_call_target="tpu_custom_call" | custom-call | tf_op jit(solution)/shard_map/final/pallas_call | solution.py:927
  (35 shorter events, 0.1 us)
Async XLA Ops:
  0.6 1.0 %copy-start = (f32[6,20,512]{2,1,0:T(8,128)S(1)}, f32[6,20,512]{2,1,0:T(8,128)}, u32[]{:S(2)}) copy-start(f32[6,20,512]{2,1,0:T(8,128)} %refs_4_.3) | copy-start | bytes 737284
  1.6 0.7 copy-start.15
  2.3 9.5 %copy-start.2 = (f32[6,20,512]{2,1,0:T(8,128)S(1)}, f32[6,20,512]{2,1,0:T(8,128)}, u32[]{:S(2)}) copy-start(f32[6,20,512]{2,1,0:T(8,128)} %refs_5_.3) | copy-start | bytes 737284
  2.3 9.5 %copy-start.3 = (f32[32,12,32]{2,0,1:T(8,128)S(1)}, f32[32,12,32]{2,0,1:T(8,128)}, u32[]{:S(2)}) copy-start(f32[32,12,32]{2,0,1:T(8,128)} %param.39) | copy-start | bytes 147460
  2.3 9.5 %copy-start.4 = (f32[2,23,512]{2,0,1:T(2,128)S(1)}, f32[2,23,512]{2,0,1:T(2,128)}, u32[]{:S(2)}) copy-start(f32[2,23,512]{2,0,1:T(2,128)} %param.36) | copy-start | bytes 282628
  2.3 9.5 %copy-start.5 = (f32[3,20,20]{2,1,0:T(8,128)S(1)}, f32[3,20,20]{2,1,0:T(8,128)}, u32[]{:S(2)}) copy-start(f32[3,20,20]{2,1,0:T(8,128)} %refs_5_.2) | copy-start | bytes 14404
  2.3 9.6 %copy-start.6 = (f32[9,512]{1,0:T(8,128)S(1)}, f32[9,512]{1,0:T(8,128)}, u32[]{:S(2)}) copy-start(f32[9,512]{1,0:T(8,128)} %refs_7_.3) | copy-start | bytes 55300
  2.3 9.6 %copy-start.7 = (f32[3,4,512]{2,1,0:T(4,128)S(1)}, f32[3,4,512]{2,1,0:T(4,128)}, u32[]{:S(2)}) copy-start(f32[3,4,512]{2,1,0:T(4,128)} %refs_8_.3) | copy-start | bytes 73732
  2.3 9.6 %copy-start.8 = (f32[23,20]{1,0:T(8,128)S(1)}, f32[23,20]{1,0:T(8,128)}, u32[]{:S(2)}) copy-start(f32[23,20]{1,0:T(8,128)} %refs_9_.2) | copy-start | bytes 5524
  2.3 9.6 %copy-start.9 = (f32[20,23]{1,0:T(8,128)S(1)}, f32[20,23]{1,0:T(8,128)}, u32[]{:S(2)}) copy-start(f32[20,23]{1,0:T(8,128)} %refs_10_.1) | copy-start | bytes 5524
  2.3 9.6 %copy-start.10 = (f32[20,40]{1,0:T(8,128)S(1)}, f32[20,40]{1,0:T(8,128)}, u32[]{:S(2)}) copy-start(f32[20,40]{1,0:T(8,128)} %refs_11_.1) | copy-start | bytes 9604
  2.3 9.6 %copy-start.11 = (s32[4,512]{1,0:T(4,128)S(1)}, s32[4,512]{1,0:T(4,128)}, u32[]{:S(2)}) copy-start(s32[4,512]{1,0:T(4,128)} %refs_6_.3) | copy-start | bytes 24580
  2.4 9.6 %copy-start.12 = (f32[4,512]{1,0:T(4,128)S(1)}, f32[4,512]{1,0:T(4,128)}, u32[]{:S(2)}) copy-start(f32[4,512]{1,0:T(4,128)} %refs_9_.3) | copy-start | bytes 24580
  2.4 9.6 %copy-start.13 = (f32[3,32]{1,0:T(4,128)S(1)}, f32[3,32]{1,0:T(4,128)}, u32[]{:S(2)}) copy-start(f32[3,32]{1,0:T(4,128)} %refs_15_.1) | copy-start | bytes 1156
  2.4 9.6 %copy-start.14 = (s32[512]{0:T(512)S(1)}, s32[512]{0:T(512)}, u32[]{:S(2)}) copy-start(s32[512]{0:T(512)} %param.35) | copy-start | bytes 6148
  2.4 9.6 %copy-start.16 = (f32[2,6]{1,0:T(2,128)S(1)}, f32[2,6]{1,0:T(2,128)}, u32[]{:S(2)}) copy-start(f32[2,6]{1,0:T(2,128)} %refs_0_.5) | copy-start | bytes 148
  2.4 9.6 %copy-start.17 = (f32[32]{0:T(128)S(1)}, f32[32]{0:T(128)}, u32[]{:S(2)}) copy-start(f32[32]{0:T(128)} %refs_0_.4) | copy-start | bytes 388
  2.4 9.6 %copy-start.18 = (s32[32]{0:T(128)S(1)}, s32[32]{0:T(128)}, u32[]{:S(2)}) copy-start(s32[32]{0:T(128)} %param.40) | copy-start | bytes 388
  2.4 9.6 %copy-start.21 = (f32[40,192]{1,0:T(8,128)S(1)}, f32[40,192]{1,0:T(8,128)}, u32[]{:S(2)}) copy-start(f32[40,192]{1,0:T(8,128)} %constant.10.clone.refs_16_) | copy-start | bytes 92164
  2.4 9.5 %copy-start.22 = (f32[32,256]{1,0:T(8,128)S(1)}, f32[32,256]{1,0:T(8,128)}, u32[]{:S(2)}) copy-start(f32[32,256]{1,0:T(8,128)} %constant.13.clone.refs_19_.refs_13_) | copy-start | bytes 98308
  2.4 9.5 %copy-start.23 = (f32[16,512]{1,0:T(8,128)S(1)}, f32[16,512]{1,0:T(8,128)}, u32[]{:S(2)}) copy-start(f32[16,512]{1,0:T(8,128)} %constant.12.clone.refs_18_.refs_14_) | copy-start | bytes 98308
  2.5 9.5 %copy-start.25 = (f32[23,96]{1,0:T(8,128)S(1)}, f32[23,96]{1,0:T(8,128)}, u32[]{:S(2)}) copy-start(f32[23,96]{1,0:T(8,128)} %constant.11.clone.refs_17_) | copy-start | bytes 26500
  3.4 14.1 %collective-permute-start = (f32[96,128]{1,0:T(8,128)S(1)}, f32[96,128]{1,0:T(8,128)S(1)}, u32[]{:S(2)}, u32[]{:S(2)}) collective-permute-start(f32[96,128]{1,0:T(8,128)S(1)} %get-tuple-element.29), channel_id=1, source_target_pairs={{0,1},{1,2},{2,3},{3,4},{4,5},{5,6},{6,7},{7,8},{8,9},{9,10},{10,1... | collective-permute-start | bytes 147464 | tf_op jit(solution)/shard_map/ppermute | solution.py:777
  7.4 10.1 %collective-permute-start.1 = (f32[96,128]{1,0:T(8,128)S(1)}, f32[96,128]{1,0:T(8,128)S(1)}, u32[]{:S(2)}, u32[]{:S(2)}) collective-permute-start(f32[96,128]{1,0:T(8,128)S(1)} %get-tuple-element.30), channel_id=1, source_target_pairs={{1,0},{2,1},{3,2},{4,3},{5,4},{6,5},{7,6},{8,7},{9,8},{10,9},{11,1... | collective-permute-start | bytes 147464 | tf_op jit(solution)/shard_map/ppermute | solution.py:778
  12.0 5.5 %copy-start.19 = (s32[32,1]{0,1:T(1,128)S(1)}, s32[32,1]{0,1:T(1,128)}, u32[]{:S(2)}) copy-start(s32[32,1]{0,1:T(1,128)} %param.41) | copy-start | bytes 388
  12.0 5.5 %copy-start.20 = (f32[32]{0:T(128)S(1)}, f32[32]{0:T(128)}, u32[]{:S(2)}) copy-start(f32[32]{0:T(128)} %param.44) | copy-start | bytes 388
  12.0 5.5 %copy-start.24 = (f32[32,4]{1,0:T(8,128)S(1)}, f32[32,4]{1,0:T(8,128)}, u32[]{:S(2)}) copy-start(f32[32,4]{1,0:T(8,128)} %constant.14.clone.refs_12_) | copy-start | bytes 1540
  17.6 13.0 %copy-start.1 = (f32[6,20,512]{2,1,0:T(8,128)S(1)}, f32[6,20,512]{2,1,0:T(8,128)}, u32[]{:S(2)}) copy-start(f32[6,20,512]{2,1,0:T(8,128)} %refs_4_.3) | copy-start | bytes 737284
  20.3 24.3 %all-to-all-start = ((f32[64,1,1408]{2,1,0:T(1,128)}), f32[64,1,1408]{2,1,0:T(1,128)S(1)}, u32[]{:S(2)}, u32[]{:S(2)}) async-start(f32[64,1,1408]{2,1,0:T(1,128)} %bitcast.7), calls=%async_computation | async-start | bytes 720896 | tf_op jit(solution)/shard_map/all_to_all | solution.py:906
